TPU v7x, 128 devices: a whole 4x4x4 slice. The times are simulated.
128 devices in a mesh: ctx: 64 (over x_hi, z, y, core), head: 2 (over x_lo).
Axes of the slice: x: 4 (x_hi: 2, x_lo: 2; x = x_hi * 2 + x_lo), y: 4, z: 4, core: 2. Of those that a mesh axis runs over, the one named last changes fastest.
Arguments:
- hidden_states: bfloat16 [32768, 5376], P('ctx', 'head'), may hold values from -6 to 6
- query_base: bfloat16 [32768, 4096], P('ctx', 'head'), may hold values from -8 to 8
- key_base: bfloat16 [32768, 2048], P('ctx', 'head'), may hold values from -8 to 8
- frozen_value_rows: bfloat16 [32768, 2048], P('ctx', 'head'), may hold values from -6 to 6
- query_down: bfloat16 [5376, 16], P('head'), may hold values from -0.078125 to 0.078125
- query_up: bfloat16 [16, 4096], P(None, 'head'), may hold values from -0.75 to 0.75
- value_down: bfloat16 [5376, 16], P('head'), may hold values from -0.078125 to 0.078125
- value_up_weight: bfloat16 [16, 2048], P(None, 'head'), may hold values from -0.75 to 0.75
- positions: int32 [32768], P('ctx'), may hold values from 0 to 65534, as said below
- block_mask: int32 [256, 9], replicated, may hold values from 0 to 1, as said below
- output_gradient: bfloat16 [32768, 4096], P('ctx', 'head'), may hold values from -96 to 96
Outputs:
- attention_out: bfloat16 [32768, 4096], P('ctx', 'head')
- grad_query_down: float32 [5376, 16], P('head')
- grad_query_up: float32 [16, 4096], P(None, 'head')
- grad_value_down: float32 [5376, 16], P('head')
- grad_value_up: float32 [16, 2048], P(None, 'head')
Inputs may be any that keep to these rules, and one draw needn't show every extreme that they name: positions rise strictly along the tokens. `block_mask`: entry (b, o) is 1 where the query block b may attend the key block b - o; column 0 is 1 in every row.
All inputs are finite; a program needn't handle non-finite values.
Results may differ from a plain program's by a relative error of at most 0.04.
Values may be sent and summed in bfloat16 or wider, within the bound.
A program may use at most 192 MiB of HBM per device.

v0:
```python
import jax
import jax.numpy as jnp
from jax import lax
from jax.sharding import PartitionSpec as P

D = 5376
QUERY_HEADS = 32
KEY_VALUE_HEADS = 16
HEAD_SIZE = 128
WINDOW = 1024
BLOCK = 128


rope_base = 10000.0


def shifted(x, axis, by):
    devices = lax.axis_size(axis)
    pairs = [(i, i + by) for i in range(devices) if 0 <= i + by < devices]
    return lax.ppermute(x, axis, pairs)


def rotate(row_block, position_ids, turn_sign):
    count = row_block.shape[0]
    col_count = row_block.shape[1]
    half_width = HEAD_SIZE // 2
    frequency = rope_base ** (-(2.0 * jnp.arange(half_width, dtype=jnp.float32)) / HEAD_SIZE)
    angles = position_ids.astype(jnp.float32)[:, None] * frequency[None, :]
    cosines = jnp.concatenate([jnp.cos(angles), jnp.cos(angles)], axis=-1)
    sines = jnp.concatenate([jnp.sin(angles), jnp.sin(angles)], axis=-1)
    shaped = row_block.reshape(count, col_count // HEAD_SIZE, HEAD_SIZE)
    turned = jnp.concatenate([-shaped[..., half_width:], shaped[..., :half_width]], axis=-1)
    return (shaped * cosines[:, None, :] + turn_sign * turned * sines[:, None, :]).reshape(
        count, col_count
    )


def allowed_pairs(mask_rows, query_first, key_first, count_of_queries, key_count):
    query_ids = query_first + jnp.arange(count_of_queries, dtype=jnp.int32)
    key_ids = key_first + jnp.arange(key_count, dtype=jnp.int32)
    token_gap = key_ids[None, :] - query_ids[:, None]
    token_ok = (token_gap <= 0) & (token_gap > -WINDOW) & (key_ids >= 0)[None, :]
    query_blocks = query_first // BLOCK + jnp.arange(count_of_queries // BLOCK, dtype=jnp.int32)
    key_blocks = key_first // BLOCK + jnp.arange(key_count // BLOCK, dtype=jnp.int32)
    offset = query_blocks[:, None] - key_blocks[None, :]
    band_size = mask_rows.shape[1]
    band_hit = jnp.any(
        (offset[:, :, None] == jnp.arange(band_size, dtype=jnp.int32)[None, None, :])
        & (mask_rows[:, None, :] == 1),
        axis=-1,
    )
    spread_out = jnp.broadcast_to(
        band_hit[:, None, :, None], (count_of_queries // BLOCK, BLOCK, key_count // BLOCK, BLOCK)
    ).reshape(count_of_queries, key_count)
    return token_ok & spread_out


def head_scores(query_rows, key_rows, head_index, score_scale):
    count_of_queries = query_rows.shape[0]
    query_groups = QUERY_HEADS // KEY_VALUE_HEADS
    head_queries = lax.dynamic_slice_in_dim(
        query_rows, head_index * query_groups * HEAD_SIZE, query_groups * HEAD_SIZE, 1
    ).reshape(count_of_queries, query_groups, HEAD_SIZE)
    head_keys = lax.dynamic_slice_in_dim(key_rows, head_index * HEAD_SIZE, HEAD_SIZE, 1)
    return (
        jnp.einsum("lgd,kd->glk", head_queries, head_keys, preferred_element_type=jnp.float32)
        * score_scale,
        head_keys,
    )


def attend(query_rows, key_rows, value_rows, allowed, score_scale):
    count_of_queries = query_rows.shape[0]
    kv_heads = key_rows.shape[1] // HEAD_SIZE
    query_groups = QUERY_HEADS // KEY_VALUE_HEADS
    group_width = query_groups * HEAD_SIZE

    def attend_one_head(head_index, loop_state):
        attn_out, log_totals = loop_state
        scores, head_keys = head_scores(query_rows, key_rows, head_index, score_scale)
        scores = jnp.where(allowed[None], scores, -jnp.inf)
        row_max = jnp.max(scores, axis=-1, keepdims=True)
        log_total = row_max[..., 0] + jnp.log(jnp.sum(jnp.exp(scores - row_max), axis=-1))
        rounded_length = jnp.exp(scores - log_total[..., None]).astype(jnp.bfloat16)
        head_values = lax.dynamic_slice_in_dim(value_rows, head_index * HEAD_SIZE, HEAD_SIZE, 1)
        head_out = jnp.einsum(
            "glk,kd->lgd", rounded_length, head_values, preferred_element_type=jnp.float32
        ).astype(jnp.bfloat16)
        attn_out = lax.dynamic_update_slice_in_dim(
            attn_out, head_out.reshape(count_of_queries, group_width), head_index * group_width, 1
        )
        log_totals = lax.dynamic_update_slice_in_dim(log_totals, log_total[None], head_index, 0)
        return (attn_out, log_totals)

    initial = (
        jnp.zeros((count_of_queries, kv_heads * group_width), jnp.bfloat16),
        jnp.zeros((kv_heads, query_groups, count_of_queries), jnp.float32),
    )
    return lax.fori_loop(0, kv_heads, attend_one_head, initial)


def backward(
    query_rows,
    key_rows,
    value_rows,
    allowed,
    log_totals,
    output_gradient,
    attention_out,
    score_scale,
):
    count_of_queries = query_rows.shape[0]
    key_count = key_rows.shape[0]
    kv_heads = key_rows.shape[1] // HEAD_SIZE
    query_groups = QUERY_HEADS // KEY_VALUE_HEADS
    group_width = query_groups * HEAD_SIZE

    def backward_one_head(head_index, loop_state):
        query_sums, value_sums = loop_state
        scores, head_keys = head_scores(query_rows, key_rows, head_index, score_scale)
        log_total = lax.dynamic_index_in_dim(log_totals, head_index, 0, keepdims=False)
        weights = jnp.exp(jnp.where(allowed[None], scores, -jnp.inf) - log_total[..., None])
        rounded_length = weights.astype(jnp.bfloat16)
        head_values = lax.dynamic_slice_in_dim(value_rows, head_index * HEAD_SIZE, HEAD_SIZE, 1)
        head_grads = lax.dynamic_slice_in_dim(
            output_gradient, head_index * group_width, group_width, 1
        ).reshape(count_of_queries, query_groups, HEAD_SIZE)
        head_outs = lax.dynamic_slice_in_dim(
            attention_out, head_index * group_width, group_width, 1
        ).reshape(count_of_queries, query_groups, HEAD_SIZE)
        row_delta = jnp.sum(head_grads.astype(jnp.float32) * head_outs.astype(jnp.float32), axis=-1)
        grad_weights = jnp.einsum(
            "lgd,kd->glk", head_grads, head_values, preferred_element_type=jnp.float32
        )
        grad_scores = (weights * (grad_weights - row_delta.T[:, :, None]) * score_scale).astype(
            jnp.bfloat16
        )
        query_part = jnp.einsum(
            "glk,kd->lgd", grad_scores, head_keys, preferred_element_type=jnp.float32
        ).reshape(count_of_queries, group_width)
        value_portion = jnp.einsum(
            "glk,lgd->kd", rounded_length, head_grads, preferred_element_type=jnp.float32
        )
        query_sums = lax.dynamic_update_slice_in_dim(
            query_sums, query_part, head_index * group_width, 1
        )
        value_sums = lax.dynamic_update_slice_in_dim(
            value_sums, value_portion, head_index * HEAD_SIZE, 1
        )
        return (query_sums, value_sums)

    initial = (
        jnp.zeros((count_of_queries, kv_heads * group_width), jnp.float32),
        jnp.zeros((key_count, kv_heads * HEAD_SIZE), jnp.float32),
    )
    return lax.fori_loop(0, kv_heads, backward_one_head, initial)


def per_device(
    hidden_states,
    query_base,
    key_base,
    frozen_value_rows,
    query_down,
    query_up,
    value_down,
    value_up_weight,
    positions,
    block_mask,
    output_gradient,
):
    count_of_queries = hidden_states.shape[0]
    key_extent = WINDOW // count_of_queries
    key_range_length = (key_extent + 1) * count_of_queries
    score_scale = (D // QUERY_HEADS) ** (-0.5)
    mask_height = count_of_queries // BLOCK
    device_index = lax.axis_index("ctx")
    leading_token = device_index * count_of_queries
    tokens_all = count_of_queries * lax.axis_size("ctx")
    query_sum, value_sum = lax.psum(
        (
            jnp.dot(hidden_states, query_down, preferred_element_type=jnp.float32),
            jnp.dot(hidden_states, value_down, preferred_element_type=jnp.float32),
        ),
        "head",
    )
    query_low = query_sum.astype(jnp.bfloat16)
    value_low = value_sum.astype(jnp.bfloat16)
    query_rows = rotate(
        query_base.astype(jnp.float32)
        + jnp.dot(query_low, query_up, preferred_element_type=jnp.float32),
        positions,
        1.0,
    ).astype(jnp.bfloat16)
    key_rows = rotate(key_base.astype(jnp.float32), positions, 1.0).astype(jnp.bfloat16)
    values = (
        frozen_value_rows.astype(jnp.float32)
        + jnp.dot(value_low, value_up_weight, preferred_element_type=jnp.float32)
    ).astype(jnp.bfloat16)
    earlier = []
    for distance in range(key_extent, 0, -1):
        earlier.append(shifted((key_rows, values), "ctx", distance))
    window_key_rows = jnp.concatenate([pair[0] for pair in earlier] + [key_rows], axis=0)
    window_value_rows = jnp.concatenate([pair[1] for pair in earlier] + [values], axis=0)
    own_mask = lax.dynamic_slice_in_dim(block_mask, device_index * mask_height, mask_height, 0)
    allowed = allowed_pairs(
        own_mask,
        leading_token,
        leading_token - key_extent * count_of_queries,
        count_of_queries,
        key_range_length,
    )
    attention_out, log_totals = attend(
        query_rows, window_key_rows, window_value_rows, allowed, score_scale
    )
    query_sums, value_sums = backward(
        query_rows,
        window_key_rows,
        window_value_rows,
        allowed,
        log_totals,
        output_gradient,
        attention_out,
        score_scale,
    )
    value_total = value_sums[key_extent * count_of_queries :]
    for distance in range(1, key_extent + 1):
        partial_value = value_sums[
            (key_extent - distance)
            * count_of_queries : (key_extent - distance + 1)
            * count_of_queries
        ]
        value_total = value_total + shifted(partial_value, "ctx", -distance)
    query_grad = rotate(query_sums, positions, -1.0).astype(jnp.bfloat16)
    value_grad = value_total.astype(jnp.bfloat16)
    contract_cols = (((1,), (1,)), ((), ()))
    contract_rows = (((0,), (0,)), ((), ()))
    query_part = lax.dot_general(
        query_grad, query_up, contract_cols, preferred_element_type=jnp.float32
    )
    value_portion = lax.dot_general(
        value_grad, value_up_weight, contract_cols, preferred_element_type=jnp.float32
    )
    query_back_sum, value_back_sum = lax.psum((query_part, value_portion), "head")
    query_back = query_back_sum.astype(jnp.bfloat16)
    value_back = value_back_sum.astype(jnp.bfloat16)
    down_query = lax.dot_general(
        hidden_states, query_back, contract_rows, preferred_element_type=jnp.float32
    )
    down_value = lax.dot_general(
        hidden_states, value_back, contract_rows, preferred_element_type=jnp.float32
    )
    up_query = lax.dot_general(
        query_low, query_grad, contract_rows, preferred_element_type=jnp.float32
    )
    up_value = lax.dot_general(
        value_low, value_grad, contract_rows, preferred_element_type=jnp.float32
    )
    summed = lax.psum((down_query, up_query, down_value, up_value), "ctx")
    loss_scale = tokens_all ** (-0.5)
    return (
        attention_out,
        summed[0] * loss_scale,
        summed[1] * loss_scale,
        summed[2] * loss_scale,
        summed[3] * loss_scale,
    )


def solution(mesh):
    placed = (
        P("ctx", "head"),
        P("ctx", "head"),
        P("ctx", "head"),
        P("ctx", "head"),
        P("head", None),
        P(None, "head"),
        P("head", None),
        P(None, "head"),
        P("ctx"),
        P(),
        P("ctx", "head"),
    )
    return jax.shard_map(
        per_device,
        mesh=mesh,
        in_specs=placed,
        out_specs=(
            P("ctx", "head"),
            P("head", None),
            P(None, "head"),
            P("head", None),
            P(None, "head"),
        ),
        check_vma=False,
    )
```

profile of v0, /device:TPU:1, one launch (start us, length us, event | category | flops | bytes accessed | tf_op | source)
XLA Modules:
  0.0 1098.7 jit_solution(8721399696083193250)
XLA Ops:
  15.7 5.2 collective-permute-start.2
  20.9 3.0 collective-permute-start.3
  25.6 6.9 all-reduce.2
  32.5 2.8 add_convert_fusion.1
  35.3 5.0 collective-permute-start
  40.3 2.8 collective-permute-start.1
  44.8 3.3 slice_negate_fusion
  48.1 3.4 maximum_multiply_fusion
  51.8 3.9 fusion.57
  56.1 4.1 copy.49
  60.8 3.6 collective-permute-done.3
  64.4 3.2 pad_maximum_fusion.1
  67.6 9.2 collective-permute-done
  76.8 11.2 %collective-permute-done.1 = bf16[512,1024]{1,0:T(8,128)(2,1)} collective-permute-done((bf16[512,1024]{1,0:T(8,128)(2,1)}, bf16[512,1024]{1,0:T(8,128)(2,1)}, u32[]{:S(2)}, u32[]{:S(2)}) %collective-permute-start.1) | collective-permute-done | bytes 1048608 | tf_op jit(solution)/shard_map/ppermute | solution.py:20
  88.1 3.2 pad_maximum_fusion
  92.7 95.8 %while.36 = (s32[]{:T(128)}, bf16[512,2048]{0,1:T(8,128)(2,1)}, f32[8,2,512]{2,1,0:T(2,128)}, bf16[1536,1024]{1,0:T(8,128)(2,1)}, bf16[1536,1024]{1,0:T(8,128)(2...) while((s32[]{:T(128)}, bf16[512,2048]{0,1:T(8,128)(2,1)}, ...), condition=%wide.region_6.7_spmd.clone, body=%wide.region_3.6_spmd.clone.sunk | while | flops 827456512 | bytes 25995568 | solution.py:99
  101.0 3.0 fusion.123
  113.0 3.0 fusion.123
  124.9 3.0 fusion.123
  136.9 3.0 fusion.123
  148.9 3.0 fusion.123
  160.9 3.0 fusion.123
  172.9 3.0 fusion.123
  184.8 3.0 fusion.123
  188.5 3.5 broadcast_in_dim.119
  194.5 192.9 %while.37 = (s32[]{:T(128)}, f32[512,2048]{0,1:T(8,128)}, f32[1536,1024]{1,0:T(8,128)}, bf16[1536,1024]{1,0:T(8,128)(2,1)}, bf16[512,2048]{0,1:T(8,128)(2,1)}, /...) while((s32[]{:T(128)}, f32[512,2048]{0,1:T(8,128)}, ...), condition=%wide.region_9.10_spmd.clone, body=%wide.region_7.9_spmd.clone.sunk | while | flops 1633156096 | bytes 32426892 | solution.py:156
  195.6 4.6 fusion.131
  205.0 5.2 fusion.135
  211.9 6.0 fusion.134
  219.7 4.6 fusion.131
  229.0 5.2 fusion.135
  235.9 6.0 fusion.134
  243.7 4.6 fusion.131
  253.1 5.3 fusion.135
  260.0 6.0 fusion.134
  267.8 4.6 fusion.131
  277.2 5.2 fusion.135
  284.0 6.1 fusion.134
  292.0 4.6 fusion.131
  301.3 5.3 fusion.135
  308.2 6.0 fusion.134
  316.0 4.6 fusion.131
  325.3 5.2 fusion.135
  332.2 6.0 fusion.134
  340.0 4.6 fusion.131
  349.4 5.2 fusion.135
  356.2 6.0 fusion.134
  364.1 4.6 fusion.131
  373.4 5.3 fusion.135
  380.3 6.2 fusion.134
  387.3 4.9 fusion.70
  395.4 5.7 copy.54
  401.1 4.9 fusion.71
  406.1 4.9 copy.68
  410.9 4.5 neg.21
  415.4 4.9 copy.69
  420.3 4.7 maximum_multiply_fusion.1
  426.2 4.5 fusion.56
  432.5 8.8 collective-permute-done.4
  441.3 3.9 collective-permute-done.5
  445.2 3.4 add_convert_fusion
  449.9 7.6 all-reduce.1
  459.9 3.9 copy.57
  463.8 621.6 %all-reduce.5.cloned.1.call-done = (f32[2688,16]{0,1:T(8,128)}, f32[16,2048]{1,0:T(8,128)}, f32[2688,16]{0,1:T(8,128)}, f32[16,1024]{1,0:T(8,128)}) async-done(((f32[2688,16]{0,1:T(8,128)}, f32[16,2048]{1,0:T(8,128)}, f32[2688,16]{0,1:T(8,128)}, f32[16,1024]{1,0:T(8,128)}), (f32[2688,16]{0,1:T(8,128)}, f32[16,2048]{1,0:T(8,128)}, f32[2688,16]{0,1:T(8,128)}, ...) | async-done | bytes 540688 | tf_op jit(solution)/shard_map/psum | solution.py:259
  (230 shorter events, 170.0 us)
Async XLA Ops:
  7.2 16.7 %copy-start = (bf16[512,2688]{1,0:T(8,128)(2,1)S(1)}, bf16[512,2688]{1,0:T(8,128)(2,1)}, u32[]{:S(2)}) copy-start(bf16[512,2688]{1,0:T(8,128)(2,1)} %param.15) | copy-start | bytes 8257540
  7.2 1078.2 %all-reduce.5.cloned.1.call-start = ((), (), s32[]{:S(2)}) async-start(), calls=%async_computation | async-start | bytes 1081344 | tf_op jit(solution)/shard_map/psum | solution.py:259
  12.6 1.2 copy-start.5
  13.8 10.1 copy-start.13
  15.7 9.0 copy-start.14
  15.7 45.1 %collective-permute-start.2 = (bf16[512,1024]{1,0:T(8,128)(2,1)}, bf16[512,1024]{1,0:T(8,128)(2,1)}, u32[]{:S(2)}, u32[]{:S(2)}) collective-permute-start(bf16[512,1024]{1,0:T(8,128)(2,1)} %fusion.59), channel_id=1, source_target_pairs={{0,4},{2,6},{4,8},{6,10},{8,12},{10,14},{12,16},{14,18},{16,20},{1... | collective-permute-start | bytes 3145736 | tf_op jit(solution)/shard_map/ppermute | solution.py:20
  20.9 43.5 %collective-permute-start.3 = (bf16[512,1024]{1,0:T(8,128)(2,1)}, bf16[512,1024]{1,0:T(8,128)(2,1)}, u32[]{:S(2)}, u32[]{:S(2)}) collective-permute-start(bf16[512,1024]{1,0:T(8,128)(2,1)} %fusion.59), channel_id=1, source_target_pairs={{0,2},{2,4},{4,6},{6,8},{8,10},{10,12},{12,14},{14,16},{16,18},{18... | collective-permute-start | bytes 3145736 | tf_op jit(solution)/shard_map/ppermute | solution.py:20
  24.7 7.7 copy-start.10
  24.7 18.4 %copy-start.8 = (bf16[16,2048]{1,0:T(8,128)(2,1)S(1)}, bf16[16,2048]{1,0:T(8,128)(2,1)}, u32[]{:S(2)}) copy-start(bf16[16,2048]{1,0:T(8,128)(2,1)} %param.20) | copy-start | bytes 196612
  32.4 11.4 %copy-start.15 = (bf16[512,16]{0,1:T(8,128)(2,1)}, bf16[512,16]{0,1:T(8,128)(2,1)S(1)}, u32[]{:S(2)}) copy-start(bf16[512,16]{0,1:T(8,128)(2,1)S(1)} %get-tuple-element.623) | copy-start | bytes 49156
  32.4 11.4 %copy-start.17 = (bf16[512,16]{0,1:T(8,128)(2,1)}, bf16[512,16]{0,1:T(8,128)(2,1)S(1)}, u32[]{:S(2)}) copy-start(bf16[512,16]{0,1:T(8,128)(2,1)S(1)} %get-tuple-element.624) | copy-start | bytes 49156
  32.5 10.6 copy-start.6
  35.3 41.5 %collective-permute-start = (bf16[512,1024]{1,0:T(8,128)(2,1)}, bf16[512,1024]{1,0:T(8,128)(2,1)}, u32[]{:S(2)}, u32[]{:S(2)}) collective-permute-start(bf16[512,1024]{1,0:T(8,128)(2,1)} %add_convert_fusion.1), channel_id=1, source_target_pairs={{0,4},{2,6},{4,8},{6,10},{8,12},{10,14},{12,16},{14,18},{16,20},{1... | collective-permute-start | bytes 3145736 | tf_op jit(solution)/shard_map/ppermute | solution.py:20
  40.3 47.8 %collective-permute-start.1 = (bf16[512,1024]{1,0:T(8,128)(2,1)}, bf16[512,1024]{1,0:T(8,128)(2,1)}, u32[]{:S(2)}, u32[]{:S(2)}) collective-permute-start(bf16[512,1024]{1,0:T(8,128)(2,1)} %add_convert_fusion.1), channel_id=1, source_target_pairs={{0,2},{2,4},{4,6},{6,8},{8,10},{10,12},{12,14},{14,16},{16,18},{18... | collective-permute-start | bytes 3145736 | tf_op jit(solution)/shard_map/ppermute | solution.py:20
  51.8 3.9 copy-start.1
  51.8 3.9 copy-start.19
  204.2 6.0 copy-start.3
  205.0 5.3 copy-start.12
  228.3 6.0 copy-start.3
  229.0 5.3 copy-start.12
  252.3 6.0 copy-start.3
  253.1 5.3 copy-start.12
  276.4 6.0 copy-start.3
  277.2 5.2 copy-start.12
  300.6 6.0 copy-start.3
  301.3 5.3 copy-start.12
  324.6 6.0 copy-start.3
  325.3 5.3 copy-start.12
  348.6 6.0 copy-start.3
  349.4 5.2 copy-start.12
  372.7 6.0 copy-start.3
  373.4 5.3 copy-start.12
  392.2 49.1 %collective-permute-start.4 = (f32[512,1024]{1,0:T(8,128)}, f32[512,1024]{1,0:T(8,128)}, u32[]{:S(2)}, u32[]{:S(2)}) collective-permute-start(f32[512,1024]{1,0:T(8,128)} %get-tuple-element.629), channel_id=1, source_target_pairs={{2,0},{4,2},{6,4},{8,6},{10,8},{12,10},{14,12},{16,14},{18,16},{20... | collective-permute-start | bytes 6291464 | tf_op jit(solution)/shard_map/ppermute | solution.py:20
  394.1 51.1 %collective-permute-start.5 = (f32[512,1024]{1,0:T(8,128)}, f32[512,1024]{1,0:T(8,128)}, u32[]{:S(2)}, u32[]{:S(2)}) collective-permute-start(f32[512,1024]{1,0:T(8,128)} %get-tuple-element.630), channel_id=1, source_target_pairs={{4,0},{6,2},{8,4},{10,6},{12,8},{14,10},{16,12},{18,14},{20,16},{2... | collective-permute-start | bytes 6291464 | tf_op jit(solution)/shard_map/ppermute | solution.py:20
  415.4 4.9 copy-start.7
  420.3 4.8 copy-start.2
  420.3 5.9 copy-start.4
  426.2 4.5 copy-start.9
  426.2 5.2 copy-start.18
  432.5 16.1 %copy-start.11 = (bf16[16,1024]{1,0:T(8,128)(2,1)S(1)}, bf16[16,1024]{1,0:T(8,128)(2,1)}, u32[]{:S(2)}) copy-start(bf16[16,1024]{1,0:T(8,128)(2,1)} %param.22) | copy-start | bytes 98308
  432.5 16.5 %copy-start.16 = (bf16[512,16]{0,1:T(8,128)(2,1)S(1)}, bf16[512,16]{0,1:T(8,128)(2,1)}, u32[]{:S(2)}) copy-start(bf16[512,16]{0,1:T(8,128)(2,1)} %copy-done.15) | copy-start | bytes 49156
Sparse Core Ops, SparseCore 0:
  460.0 625.3 all-reduce.4
where the time goes:
time: 1110 us; the launch traced here: 1100 us
  waiting for transfers between devices  658 us (59%)
  matrix products  180 us (16%)
  other arithmetic  117 us (11%)
  local copies, waits for them, and re-layouts  94.5 us (9%)
  starting transfers between devices  19.2 us (2%)
  between operations  14.6 us (1%)
  blocking collectives  14.5 us (1%)
    psum x1, waiting for transfers between devices, per_device(): summed = lax.psum((down_query, up_query, down_value, up_value), 'ctx')  622 us
    dot_general x16, matrix products, head_scores(): jnp.einsum('lgd,kd->glk', head_queries, head_keys, preferred_element_type...  55.1 us
    dot_general x8, matrix products, backward_one_head(): jnp.einsum('glk,kd->lgd', grad_scores, head_keys, preferred_element_type=...  48.3 us
    dot_general x8, matrix products, backward_one_head(): jnp.einsum('glk,lgd->kd', rounded_length, head_grads, preferred_element_t...  42 us
    and x16, other arithmetic, allowed_pairs(): return token_ok & spread_out  38.9 us
    ppermute x6, waiting for transfers between devices, shifted(): return lax.ppermute(x, axis, pairs)  36.8 us
    dot_general x8, matrix products, attend_one_head(): jnp.einsum('glk,kd->lgd', rounded_length, head_values, preferred_element_...  23.7 us
  transfers between devices with their start and end apart: 7, of which 6 were waited for; matrix products, arithmetic and copies ran while one was open for 6% of the time, Pallas kernels for 0%

commit v1 on v0

--- a/solution.py
+++ b/solution.py
@@ -1,6 +1,10 @@
+import functools
+
 import jax
 import jax.numpy as jnp
 from jax import lax
+from jax.experimental import pallas as pl
+from jax.experimental.pallas import tpu as pltpu
 from jax.sharding import PartitionSpec as P
 
 D = 5376
@@ -12,6 +16,123 @@
 
 
 rope_base = 10000.0
+
+RANK = 16
+GROUP = 8
+CHUNK = 1152
+MESH = pl.DeviceIdType.MESH
+
+
+def pieces_of(widths):
+    pieces, start = [], 0
+    for which, width in enumerate(widths):
+        done = 0
+        while done < width:
+            chunk, inside = divmod(start + done, CHUNK)
+            count = min(width - done, CHUNK - inside)
+            pieces.append((which, done, chunk, inside, count))
+            done += count
+        start += width
+    return pieces
+
+
+def total_kernel(
+    widths,
+    scale,
+    parts,
+    o_0,
+    o_1,
+    o_2,
+    o_3,
+    near,
+    far,
+    final,
+    near_send,
+    near_recv,
+    far_send,
+    far_recv,
+    final_send,
+    final_recv,
+):
+    ctx, head = lax.axis_index("ctx"), lax.axis_index("head")
+    member = ctx % GROUP
+    group = ctx // GROUP
+    near_peers = [group * GROUP + (member + by) % GROUP for by in range(1, GROUP)]
+    far_peers = [((group + by) % GROUP) * GROUP + member for by in range(1, GROUP)]
+
+    barrier = pltpu.get_barrier_semaphore()
+    for peer in near_peers + far_peers:
+        pl.semaphore_signal(barrier, inc=1, device_id=(peer, head), device_id_type=MESH)
+    pl.semaphore_wait(barrier, 2 * (GROUP - 1))
+
+    def copy(source, target, send, recv, peer):
+        return pltpu.make_async_remote_copy(
+            src_ref=source,
+            dst_ref=target,
+            send_sem=send,
+            recv_sem=recv,
+            device_id=(peer, head),
+            device_id_type=MESH,
+        )
+
+    copies = []
+    for k, peer in enumerate(near_peers):
+        one = copy(
+            parts.at[peer % GROUP], near.at[k], near_send.at[k], near_recv.at[k], peer
+        )
+        one.start()
+        copies.append(one)
+    total = parts[member].astype(jnp.float32)
+    for k, one in enumerate(copies):
+        one.wait_recv()
+        total += near[k].astype(jnp.float32)
+    far[group] = total.astype(jnp.bfloat16)
+
+    far_copies = []
+    for k, peer in enumerate(far_peers):
+        one = copy(far.at[group], far.at[group], far_send.at[k], far_recv.at[k], peer)
+        one.start()
+        far_copies.append(one)
+    for one in far_copies:
+        one.wait_recv()
+    total = far[0].astype(jnp.float32)
+    for k in range(1, GROUP):
+        total += far[k].astype(jnp.float32)
+    final[member] = (total * scale).astype(jnp.bfloat16)
+
+    last_copies = []
+    for k, peer in enumerate(near_peers):
+        one = copy(final.at[member], final.at[member], final_send.at[k], final_recv.at[k], peer)
+        one.start()
+        last_copies.append(one)
+    for one in last_copies:
+        one.wait_recv()
+    outs = (o_0, o_1, o_2, o_3)
+    for which, at, chunk, inside, count in pieces_of(widths):
+        outs[which][:, at : at + count] = final[chunk, :, inside : inside + count].astype(
+            jnp.float32
+        )
+    for one in copies + far_copies + last_copies:
+        one.wait_send()
+
+
+def total_over_ctx(parts, widths, scale):
+    chunked = (GROUP, RANK, CHUNK)
+    return pl.pallas_call(
+        functools.partial(total_kernel, widths, scale),
+        out_shape=[jax.ShapeDtypeStruct((RANK, width), jnp.float32) for width in widths],
+        in_specs=[pl.BlockSpec(memory_space=pltpu.VMEM)],
+        out_specs=[pl.BlockSpec(memory_space=pltpu.VMEM)] * len(widths),
+        scratch_shapes=[
+            pltpu.VMEM((GROUP - 1, RANK, CHUNK), jnp.bfloat16),
+            pltpu.VMEM(chunked, jnp.bfloat16),
+            pltpu.VMEM(chunked, jnp.bfloat16),
+        ]
+        + [pltpu.SemaphoreType.DMA((GROUP - 1,))] * 6,
+        compiler_params=pltpu.CompilerParams(
+            collective_id=0, has_side_effects=True, vmem_limit_bytes=24 * 2**20
+        ),
+    )(parts)
 
 
 def shifted(x, axis, by):
@@ -245,10 +366,10 @@
     query_back = query_back_sum.astype(jnp.bfloat16)
     value_back = value_back_sum.astype(jnp.bfloat16)
     down_query = lax.dot_general(
-        hidden_states, query_back, contract_rows, preferred_element_type=jnp.float32
+        query_back, hidden_states, contract_rows, preferred_element_type=jnp.float32
     )
     down_value = lax.dot_general(
-        hidden_states, value_back, contract_rows, preferred_element_type=jnp.float32
+        value_back, hidden_states, contract_rows, preferred_element_type=jnp.float32
     )
     up_query = lax.dot_general(
         query_low, query_grad, contract_rows, preferred_element_type=jnp.float32
@@ -256,15 +377,14 @@
     up_value = lax.dot_general(
         value_low, value_grad, contract_rows, preferred_element_type=jnp.float32
     )
-    summed = lax.psum((down_query, up_query, down_value, up_value), "ctx")
     loss_scale = tokens_all ** (-0.5)
-    return (
-        attention_out,
-        summed[0] * loss_scale,
-        summed[1] * loss_scale,
-        summed[2] * loss_scale,
-        summed[3] * loss_scale,
-    )
+    mine = (down_query, up_query, down_value, up_value)
+    widths = tuple(part.shape[1] for part in mine)
+    row = jnp.concatenate(mine, axis=1).astype(jnp.bfloat16)
+    row = jnp.pad(row, ((0, 0), (0, GROUP * CHUNK - row.shape[1])))
+    parts = row.reshape(RANK, GROUP, CHUNK).transpose(1, 0, 2)
+    down_query, up_query, down_value, up_value = total_over_ctx(parts, widths, loss_scale)
+    return attention_out, down_query.T, up_query, down_value.T, up_value
 
 
 def solution(mesh):

time: 1110 us -> 523 us (0.47)
  waiting for transfers between devices: 658 us -> 45.2 us
  Pallas kernels: 0 us -> 51.3 us
  between operations: 14.6 us -> 1.2 us
    psum x1 -> x0, waiting for transfers between devices: 622 us -> none  [per_device(): summed = lax.psum((down_query, up_query, down_value, up_value), 'ctx')]
    pallas_call x0 -> x1, Pallas kernels: none -> 51.3 us  [total_over_ctx(): pl.pallas_call(functools.partial(total_kernel, widths, scale), out_shape=...]
    unnamed x43 -> x49, local copies, waits for them, and re-layouts: 21 us -> 24.2 us
  transfers between devices with their start and end apart: 7 -> 6, of which waited for: 6 -> 5; matrix products, arithmetic and copies ran while one was open for 6% -> 10% of each run, Pallas kernels for 0% -> 0%
where the time goes in v1:
time: 523 us; the launch traced here: 514 us
  matrix products  177 us (34%)
  other arithmetic  110 us (21%)
  local copies, waits for them, and re-layouts  95.3 us (18%)
  Pallas kernels  51.3 us (10%)
  waiting for transfers between devices  45.2 us (9%)
  starting transfers between devices  18.9 us (4%)
  blocking collectives  14.5 us (3%)
    dot_general x16, matrix products, head_scores(): jnp.einsum('lgd,kd->glk', head_queries, head_keys, preferred_element_type...  55.1 us
    pallas_call x1, Pallas kernels, total_over_ctx(): pl.pallas_call(functools.partial(total_kernel, widths, scale), out_shape=...  51.3 us
    dot_general x8, matrix products, backward_one_head(): jnp.einsum('glk,kd->lgd', grad_scores, head_keys, preferred_element_type=...  48.1 us
    ppermute x6, waiting for transfers between devices, shifted(): return lax.ppermute(x, axis, pairs)  45.2 us
    dot_general x8, matrix products, backward_one_head(): jnp.einsum('glk,lgd->kd', rounded_length, head_grads, preferred_element_t...  42 us
    and x16, other arithmetic, allowed_pairs(): return token_ok & spread_out  38.6 us
    unnamed x49, local copies, waits for them, and re-layouts  24.2 us
    dot_general x8, matrix products, attend_one_head(): jnp.einsum('glk,kd->lgd', rounded_length, head_values, preferred_element_...  23.7 us
  transfers between devices with their start and end apart: 6, of which 5 were waited for; matrix products, arithmetic and copies ran while one was open for 10% of the time, Pallas kernels for 0%

profile of v1, /device:TPU:1, one launch (start us, length us, event | category | flops | bytes accessed | tf_op | source)
XLA Modules:
  0.0 514.5 jit_solution(10491393325707216493)
XLA Ops:
  9.1 5.2 %collective-permute-start.2 = (bf16[512,1024]{1,0:T(8,128)(2,1)}, bf16[512,1024]{1,0:T(8,128)(2,1)}, u32[]{:S(2)}, u32[]{:S(2)}) collective-permute-start(bf16[512,1024]{1,0:T(8,128)(2,1)} %fusion.59), channel_id=1, source_target_pairs={{0,4},{2,6},{4,8},{6,10},{8,12},{10,14},{12,16},{14,18},{16,20},{1... | collective-permute-start | bytes 3145736 | tf_op jit(solution)/shard_map/ppermute | solution.py:141
  14.3 3.0 collective-permute-start.3
  19.0 6.9 %all-reduce.2 = (bf16[512,16]{0,1:T(8,128)(2,1)S(1)}, bf16[512,16]{0,1:T(8,128)(2,1)S(1)}) all-reduce(f32[512,16]{0,1:T(8,128)S(1)} %fusion.77, f32[512,16]{0,1:T(8,128)S(1)} %fusion.78), channel_id=1, replica_groups=mesh['ctx'=64,'head'=2] {'head'}, use_global_device_ids=true, to_apply=%region_2.3 | all-reduce | flops 16384 | bytes 98304 | tf_op jit(solution)/shard_map/psum | solution.py:301
  25.9 2.8 add_convert_fusion.1
  28.7 5.0 collective-permute-start
  33.7 2.5 collective-permute-start.1
  38.0 3.3 slice_negate_fusion
  41.3 3.4 maximum_multiply_fusion
  45.0 3.9 fusion.57
  49.3 4.5 copy.50
  54.4 3.5 collective-permute-done.3
  57.9 3.2 pad_maximum_fusion.1
  61.1 9.2 %collective-permute-done = bf16[512,1024]{1,0:T(8,128)(2,1)} collective-permute-done((bf16[512,1024]{1,0:T(8,128)(2,1)}, bf16[512,1024]{1,0:T(8,128)(2,1)}, u32[]{:S(2)}, u32[]{:S(2)}) %collective-permute-start) | collective-permute-done | bytes 1048608 | tf_op jit(solution)/shard_map/ppermute | solution.py:141
  70.3 11.2 %collective-permute-done.1 = bf16[512,1024]{1,0:T(8,128)(2,1)} collective-permute-done((bf16[512,1024]{1,0:T(8,128)(2,1)}, bf16[512,1024]{1,0:T(8,128)(2,1)}, u32[]{:S(2)}, u32[]{:S(2)}) %collective-permute-start.1) | collective-permute-done | bytes 1048608 | tf_op jit(solution)/shard_map/ppermute | solution.py:141
  81.5 3.2 pad_maximum_fusion
  86.2 95.7 %while.36 = (s32[]{:T(128)}, bf16[512,2048]{0,1:T(8,128)(2,1)}, f32[8,2,512]{2,1,0:T(2,128)}, bf16[1536,1024]{1,0:T(8,128)(2,1)}, bf16[1536,1024]{1,0:T(8,128)(2...) while((s32[]{:T(128)}, bf16[512,2048]{0,1:T(8,128)(2,1)}, ...), condition=%wide.region_6.7_spmd.clone, body=%wide.region_3.6_spmd.clone.sunk | while | flops 827456512 | bytes 25995568 | solution.py:220
  94.4 3.0 fusion.126
  106.4 3.0 fusion.126
  118.4 3.0 fusion.126
  130.3 3.0 fusion.126
  142.3 3.0 fusion.126
  154.3 3.0 fusion.126
  166.2 3.0 fusion.126
  178.1 3.0 fusion.126
  181.9 3.9 copy.59
  185.8 3.5 broadcast_in_dim.119
  191.7 192.4 %while.37 = (s32[]{:T(128)}, f32[512,2048]{0,1:T(8,128)}, f32[1536,1024]{1,0:T(8,128)}, bf16[1536,1024]{1,0:T(8,128)(2,1)}, bf16[512,2048]{0,1:T(8,128)(2,1)}, /...) while((s32[]{:T(128)}, f32[512,2048]{0,1:T(8,128)}, ...), condition=%wide.region_9.10_spmd.clone, body=%wide.region_7.9_spmd.clone.sunk | while | flops 1633156096 | bytes 32426892 | solution.py:277
  192.8 4.6 fusion.134
  202.1 5.3 %fusion.138 = f32[1536,1024]{1,0:T(8,128)} fusion(f32[1536,1024]{1,0:T(8,128)} %get-tuple-element.863, s32[]{:T(128)S(6)} %select_n.162, bf16[512,2,128]{0,2,1:T(8,128)(2,1)S(1)} %bitcast.225, f32[1536,512,2]{1,0,2:T(8,128)} %fusion.134, f32[2,512]{1,0:T(2,128)S(1)} %dynamic-slice_bitcast_fusion.2, pred[512,1536]{0,1:T(8,128)(4,1)S(1)} %fusion.136), kind=kOutput, calls=%fused_computation.43.clone.1 | convolution fusion | flops 408944640 | bytes 8130564 | tf_op jit(solution)/shard_map/while/body/eval_jaxpr/glk,lgd->kd/dot_general | solution.py:262
  209.0 6.0 %fusion.137 = f32[128,2,512]{2,0,1:T(8,128)S(1)} fusion(f32[1536,512,2]{1,0,2:T(8,128)} %fusion.134, bf16[512,2,128]{0,2,1:T(8,128)(2,1)S(1)} %bitcast.226, f32[2,512]{1,0:T(2,128)} %bitcast.236, f32[2,512]{1,0:T(2,128)} %copy-done.13, pred[512,1536]{0,1:T(8,128)(4,1)} %copy-done.4, bf16[1536,1024]{1,0:T(8,128)(2,1)} %get-tuple-element.886, ...), kind=kOutput, calls=%fused_computation.44.clone.1 | convolution fusion | flops 816316416 | bytes 8659968 | tf_op jit(solution)/shard_map/while/body/eval_jaxpr/glk,kd->lgd/dot_general | solution.py:259
  216.9 4.6 fusion.134
  226.2 5.2 %fusion.138 = f32[1536,1024]{1,0:T(8,128)} fusion(f32[1536,1024]{1,0:T(8,128)} %get-tuple-element.863, s32[]{:T(128)S(6)} %select_n.162, bf16[512,2,128]{0,2,1:T(8,128)(2,1)S(1)} %bitcast.225, f32[1536,512,2]{1,0,2:T(8,128)} %fusion.134, f32[2,512]{1,0:T(2,128)S(1)} %dynamic-slice_bitcast_fusion.2, pred[512,1536]{0,1:T(8,128)(4,1)S(1)} %fusion.136), kind=kOutput, calls=%fused_computation.43.clone.1 | convolution fusion | flops 408944640 | bytes 8130564 | tf_op jit(solution)/shard_map/while/body/eval_jaxpr/glk,lgd->kd/dot_general | solution.py:262
  233.0 6.0 %fusion.137 = f32[128,2,512]{2,0,1:T(8,128)S(1)} fusion(f32[1536,512,2]{1,0,2:T(8,128)} %fusion.134, bf16[512,2,128]{0,2,1:T(8,128)(2,1)S(1)} %bitcast.226, f32[2,512]{1,0:T(2,128)} %bitcast.236, f32[2,512]{1,0:T(2,128)} %copy-done.13, pred[512,1536]{0,1:T(8,128)(4,1)} %copy-done.4, bf16[1536,1024]{1,0:T(8,128)(2,1)} %get-tuple-element.886, ...), kind=kOutput, calls=%fused_computation.44.clone.1 | convolution fusion | flops 816316416 | bytes 8659968 | tf_op jit(solution)/shard_map/while/body/eval_jaxpr/glk,kd->lgd/dot_general | solution.py:259
  240.9 4.6 fusion.134
  250.2 5.3 %fusion.138 = f32[1536,1024]{1,0:T(8,128)} fusion(f32[1536,1024]{1,0:T(8,128)} %get-tuple-element.863, s32[]{:T(128)S(6)} %select_n.162, bf16[512,2,128]{0,2,1:T(8,128)(2,1)S(1)} %bitcast.225, f32[1536,512,2]{1,0,2:T(8,128)} %fusion.134, f32[2,512]{1,0:T(2,128)S(1)} %dynamic-slice_bitcast_fusion.2, pred[512,1536]{0,1:T(8,128)(4,1)S(1)} %fusion.136), kind=kOutput, calls=%fused_computation.43.clone.1 | convolution fusion | flops 408944640 | bytes 8130564 | tf_op jit(solution)/shard_map/while/body/eval_jaxpr/glk,lgd->kd/dot_general | solution.py:262
  257.1 6.0 %fusion.137 = f32[128,2,512]{2,0,1:T(8,128)S(1)} fusion(f32[1536,512,2]{1,0,2:T(8,128)} %fusion.134, bf16[512,2,128]{0,2,1:T(8,128)(2,1)S(1)} %bitcast.226, f32[2,512]{1,0:T(2,128)} %bitcast.236, f32[2,512]{1,0:T(2,128)} %copy-done.13, pred[512,1536]{0,1:T(8,128)(4,1)} %copy-done.4, bf16[1536,1024]{1,0:T(8,128)(2,1)} %get-tuple-element.886, ...), kind=kOutput, calls=%fused_computation.44.clone.1 | convolution fusion | flops 816316416 | bytes 8659968 | tf_op jit(solution)/shard_map/while/body/eval_jaxpr/glk,kd->lgd/dot_general | solution.py:259
  264.9 4.6 fusion.134
  274.2 5.2 %fusion.138 = f32[1536,1024]{1,0:T(8,128)} fusion(f32[1536,1024]{1,0:T(8,128)} %get-tuple-element.863, s32[]{:T(128)S(6)} %select_n.162, bf16[512,2,128]{0,2,1:T(8,128)(2,1)S(1)} %bitcast.225, f32[1536,512,2]{1,0,2:T(8,128)} %fusion.134, f32[2,512]{1,0:T(2,128)S(1)} %dynamic-slice_bitcast_fusion.2, pred[512,1536]{0,1:T(8,128)(4,1)S(1)} %fusion.136), kind=kOutput, calls=%fused_computation.43.clone.1 | convolution fusion | flops 408944640 | bytes 8130564 | tf_op jit(solution)/shard_map/while/body/eval_jaxpr/glk,lgd->kd/dot_general | solution.py:262
  281.1 6.0 %fusion.137 = f32[128,2,512]{2,0,1:T(8,128)S(1)} fusion(f32[1536,512,2]{1,0,2:T(8,128)} %fusion.134, bf16[512,2,128]{0,2,1:T(8,128)(2,1)S(1)} %bitcast.226, f32[2,512]{1,0:T(2,128)} %bitcast.236, f32[2,512]{1,0:T(2,128)} %copy-done.13, pred[512,1536]{0,1:T(8,128)(4,1)} %copy-done.4, bf16[1536,1024]{1,0:T(8,128)(2,1)} %get-tuple-element.886, ...), kind=kOutput, calls=%fused_computation.44.clone.1 | convolution fusion | flops 816316416 | bytes 8659968 | tf_op jit(solution)/shard_map/while/body/eval_jaxpr/glk,kd->lgd/dot_general | solution.py:259
  288.9 4.6 fusion.134
  298.2 5.3 %fusion.138 = f32[1536,1024]{1,0:T(8,128)} fusion(f32[1536,1024]{1,0:T(8,128)} %get-tuple-element.863, s32[]{:T(128)S(6)} %select_n.162, bf16[512,2,128]{0,2,1:T(8,128)(2,1)S(1)} %bitcast.225, f32[1536,512,2]{1,0,2:T(8,128)} %fusion.134, f32[2,512]{1,0:T(2,128)S(1)} %dynamic-slice_bitcast_fusion.2, pred[512,1536]{0,1:T(8,128)(4,1)S(1)} %fusion.136), kind=kOutput, calls=%fused_computation.43.clone.1 | convolution fusion | flops 408944640 | bytes 8130564 | tf_op jit(solution)/shard_map/while/body/eval_jaxpr/glk,lgd->kd/dot_general | solution.py:262
  305.1 6.0 %fusion.137 = f32[128,2,512]{2,0,1:T(8,128)S(1)} fusion(f32[1536,512,2]{1,0,2:T(8,128)} %fusion.134, bf16[512,2,128]{0,2,1:T(8,128)(2,1)S(1)} %bitcast.226, f32[2,512]{1,0:T(2,128)} %bitcast.236, f32[2,512]{1,0:T(2,128)} %copy-done.13, pred[512,1536]{0,1:T(8,128)(4,1)} %copy-done.4, bf16[1536,1024]{1,0:T(8,128)(2,1)} %get-tuple-element.886, ...), kind=kOutput, calls=%fused_computation.44.clone.1 | convolution fusion | flops 816316416 | bytes 8659968 | tf_op jit(solution)/shard_map/while/body/eval_jaxpr/glk,kd->lgd/dot_general | solution.py:259
  313.0 4.6 fusion.134
  322.3 5.2 %fusion.138 = f32[1536,1024]{1,0:T(8,128)} fusion(f32[1536,1024]{1,0:T(8,128)} %get-tuple-element.863, s32[]{:T(128)S(6)} %select_n.162, bf16[512,2,128]{0,2,1:T(8,128)(2,1)S(1)} %bitcast.225, f32[1536,512,2]{1,0,2:T(8,128)} %fusion.134, f32[2,512]{1,0:T(2,128)S(1)} %dynamic-slice_bitcast_fusion.2, pred[512,1536]{0,1:T(8,128)(4,1)S(1)} %fusion.136), kind=kOutput, calls=%fused_computation.43.clone.1 | convolution fusion | flops 408944640 | bytes 8130564 | tf_op jit(solution)/shard_map/while/body/eval_jaxpr/glk,lgd->kd/dot_general | solution.py:262
  329.1 6.0 %fusion.137 = f32[128,2,512]{2,0,1:T(8,128)S(1)} fusion(f32[1536,512,2]{1,0,2:T(8,128)} %fusion.134, bf16[512,2,128]{0,2,1:T(8,128)(2,1)S(1)} %bitcast.226, f32[2,512]{1,0:T(2,128)} %bitcast.236, f32[2,512]{1,0:T(2,128)} %copy-done.13, pred[512,1536]{0,1:T(8,128)(4,1)} %copy-done.4, bf16[1536,1024]{1,0:T(8,128)(2,1)} %get-tuple-element.886, ...), kind=kOutput, calls=%fused_computation.44.clone.1 | convolution fusion | flops 816316416 | bytes 8659968 | tf_op jit(solution)/shard_map/while/body/eval_jaxpr/glk,kd->lgd/dot_general | solution.py:259
  337.0 4.6 fusion.134
  346.3 5.2 %fusion.138 = f32[1536,1024]{1,0:T(8,128)} fusion(f32[1536,1024]{1,0:T(8,128)} %get-tuple-element.863, s32[]{:T(128)S(6)} %select_n.162, bf16[512,2,128]{0,2,1:T(8,128)(2,1)S(1)} %bitcast.225, f32[1536,512,2]{1,0,2:T(8,128)} %fusion.134, f32[2,512]{1,0:T(2,128)S(1)} %dynamic-slice_bitcast_fusion.2, pred[512,1536]{0,1:T(8,128)(4,1)S(1)} %fusion.136), kind=kOutput, calls=%fused_computation.43.clone.1 | convolution fusion | flops 408944640 | bytes 8130564 | tf_op jit(solution)/shard_map/while/body/eval_jaxpr/glk,lgd->kd/dot_general | solution.py:262
  353.1 6.0 %fusion.137 = f32[128,2,512]{2,0,1:T(8,128)S(1)} fusion(f32[1536,512,2]{1,0,2:T(8,128)} %fusion.134, bf16[512,2,128]{0,2,1:T(8,128)(2,1)S(1)} %bitcast.226, f32[2,512]{1,0:T(2,128)} %bitcast.236, f32[2,512]{1,0:T(2,128)} %copy-done.13, pred[512,1536]{0,1:T(8,128)(4,1)} %copy-done.4, bf16[1536,1024]{1,0:T(8,128)(2,1)} %get-tuple-element.886, ...), kind=kOutput, calls=%fused_computation.44.clone.1 | convolution fusion | flops 816316416 | bytes 8659968 | tf_op jit(solution)/shard_map/while/body/eval_jaxpr/glk,kd->lgd/dot_general | solution.py:259
  361.0 4.6 fusion.134
  370.3 5.3 %fusion.138 = f32[1536,1024]{1,0:T(8,128)} fusion(f32[1536,1024]{1,0:T(8,128)} %get-tuple-element.863, s32[]{:T(128)S(6)} %select_n.162, bf16[512,2,128]{0,2,1:T(8,128)(2,1)S(1)} %bitcast.225, f32[1536,512,2]{1,0,2:T(8,128)} %fusion.134, f32[2,512]{1,0:T(2,128)S(1)} %dynamic-slice_bitcast_fusion.2, pred[512,1536]{0,1:T(8,128)(4,1)S(1)} %fusion.136), kind=kOutput, calls=%fused_computation.43.clone.1 | convolution fusion | flops 408944640 | bytes 8130564 | tf_op jit(solution)/shard_map/while/body/eval_jaxpr/glk,lgd->kd/dot_general | solution.py:262
  377.2 6.1 %fusion.137 = f32[128,2,512]{2,0,1:T(8,128)S(1)} fusion(f32[1536,512,2]{1,0,2:T(8,128)} %fusion.134, bf16[512,2,128]{0,2,1:T(8,128)(2,1)S(1)} %bitcast.226, f32[2,512]{1,0:T(2,128)} %bitcast.236, f32[2,512]{1,0:T(2,128)} %copy-done.13, pred[512,1536]{0,1:T(8,128)(4,1)} %copy-done.4, bf16[1536,1024]{1,0:T(8,128)(2,1)} %get-tuple-element.886, ...), kind=kOutput, calls=%fused_computation.44.clone.1 | convolution fusion | flops 816316416 | bytes 8659968 | tf_op jit(solution)/shard_map/while/body/eval_jaxpr/glk,kd->lgd/dot_general | solution.py:259
  384.1 5.4 %copy.55 = f32[512,2048]{1,0:T(8,128)} copy(f32[512,2048]{0,1:T(8,128)} %get-tuple-element.431) | data formatting | bytes 8388608 | tf_op jit(solution)/shard_map/while | solution.py:277
  389.5 5.0 fusion.75
  397.8 2.5 fusion.76
  400.3 5.1 copy.70
  405.4 4.5 neg.21
  409.9 4.9 copy.71
  414.8 4.7 maximum_multiply_fusion.1
  420.7 4.5 fusion.56
  426.3 17.4 %collective-permute-done.4 = f32[512,1024]{1,0:T(8,128)} collective-permute-done((f32[512,1024]{1,0:T(8,128)}, f32[512,1024]{1,0:T(8,128)}, u32[]{:S(2)}, u32[]{:S(2)}) %collective-permute-start.4) | collective-permute-done | bytes 2097184 | tf_op jit(solution)/shard_map/ppermute | solution.py:141
  443.6 3.9 collective-permute-done.5
  447.5 3.4 add_convert_fusion
  451.6 7.7 %all-reduce.1 = (bf16[512,16]{0,1:T(8,128)(2,1)S(1)}, bf16[512,16]{0,1:T(8,128)(2,1)S(1)}) all-reduce(f32[512,16]{0,1:T(8,128)S(1)} %fusion.80, f32[512,16]{0,1:T(8,128)S(1)} %fusion.79), channel_id=1, replica_groups=mesh['ctx'=64,'head'=2] {'head'}, use_global_device_ids=true, to_apply=%region_11.12 | all-reduce | flops 16384 | bytes 98304 | tf_op jit(solution)/shard_map/psum | solution.py:365
  460.3 51.3 %shard_map.146 = (f32[16,2688]{1,0:T(8,128)S(1)}, f32[16,2048]{1,0:T(8,128)S(1)}, f32[16,2688]{1,0:T(8,128)S(1)}, f32[16,1024]{1,0:T(8,128)S(1)}) custom-call(bf16[8,16,1152]{2,1,0:T(8,128)(2,1)S(1)} %bitcast.214), custom_call_target="tpu_custom_call" | custom-call | tf_op jit(solution)/shard_map/pallas_call | solution.py:121
  (232 shorter events, 163.4 us)
Async XLA Ops:
  0.6 16.7 %copy-start = (bf16[512,2688]{1,0:T(8,128)(2,1)S(1)}, bf16[512,2688]{1,0:T(8,128)(2,1)}, u32[]{:S(2)}) copy-start(bf16[512,2688]{1,0:T(8,128)(2,1)} %param.15) | copy-start | bytes 8257540
  6.0 1.2 copy-start.6
  7.2 10.1 %copy-start.14 = (bf16[2688,16]{0,1:T(8,128)(2,1)S(1)}, bf16[2688,16]{0,1:T(8,128)(2,1)}, u32[]{:S(2)}) copy-start(bf16[2688,16]{0,1:T(8,128)(2,1)} %param.21) | copy-start | bytes 258052
  9.1 9.0 %copy-start.15 = (bf16[2688,16]{0,1:T(8,128)(2,1)S(1)}, bf16[2688,16]{0,1:T(8,128)(2,1)}, u32[]{:S(2)}) copy-start(bf16[2688,16]{0,1:T(8,128)(2,1)} %param.19) | copy-start | bytes 258052
  9.1 45.2 %collective-permute-start.2 = (bf16[512,1024]{1,0:T(8,128)(2,1)}, bf16[512,1024]{1,0:T(8,128)(2,1)}, u32[]{:S(2)}, u32[]{:S(2)}) collective-permute-start(bf16[512,1024]{1,0:T(8,128)(2,1)} %fusion.59), channel_id=1, source_target_pairs={{0,4},{2,6},{4,8},{6,10},{8,12},{10,14},{12,16},{14,18},{16,20},{1... | collective-permute-start | bytes 3145736 | tf_op jit(solution)/shard_map/ppermute | solution.py:141
  14.3 43.5 %collective-permute-start.3 = (bf16[512,1024]{1,0:T(8,128)(2,1)}, bf16[512,1024]{1,0:T(8,128)(2,1)}, u32[]{:S(2)}, u32[]{:S(2)}) collective-permute-start(bf16[512,1024]{1,0:T(8,128)(2,1)} %fusion.59), channel_id=1, source_target_pairs={{0,2},{2,4},{4,6},{6,8},{8,10},{10,12},{12,14},{14,16},{16,18},{18... | collective-permute-start | bytes 3145736 | tf_op jit(solution)/shard_map/ppermute | solution.py:141
  18.2 7.7 %copy-start.11 = (bf16[16,1024]{1,0:T(8,128)(2,1)S(1)}, bf16[16,1024]{1,0:T(8,128)(2,1)}, u32[]{:S(2)}) copy-start(bf16[16,1024]{1,0:T(8,128)(2,1)} %param.22) | copy-start | bytes 98308
  18.2 18.1 %copy-start.9 = (bf16[16,2048]{1,0:T(8,128)(2,1)S(1)}, bf16[16,2048]{1,0:T(8,128)(2,1)}, u32[]{:S(2)}) copy-start(bf16[16,2048]{1,0:T(8,128)(2,1)} %param.20) | copy-start | bytes 196612
  25.9 11.2 %copy-start.16 = (bf16[512,16]{0,1:T(8,128)(2,1)}, bf16[512,16]{0,1:T(8,128)(2,1)S(1)}, u32[]{:S(2)}) copy-start(bf16[512,16]{0,1:T(8,128)(2,1)S(1)} %get-tuple-element.627) | copy-start | bytes 49156
  25.9 11.2 %copy-start.18 = (bf16[512,16]{0,1:T(8,128)(2,1)}, bf16[512,16]{0,1:T(8,128)(2,1)S(1)}, u32[]{:S(2)}) copy-start(bf16[512,16]{0,1:T(8,128)(2,1)S(1)} %get-tuple-element.628) | copy-start | bytes 49156
  25.9 10.4 %copy-start.7 = (bf16[512,2048]{1,0:T(8,128)(2,1)S(1)}, bf16[512,2048]{1,0:T(8,128)(2,1)}, u32[]{:S(2)}) copy-start(bf16[512,2048]{1,0:T(8,128)(2,1)} %param.16) | copy-start | bytes 6291460
  28.7 41.5 %collective-permute-start = (bf16[512,1024]{1,0:T(8,128)(2,1)}, bf16[512,1024]{1,0:T(8,128)(2,1)}, u32[]{:S(2)}, u32[]{:S(2)}) collective-permute-start(bf16[512,1024]{1,0:T(8,128)(2,1)} %add_convert_fusion.1), channel_id=1, source_target_pairs={{0,4},{2,6},{4,8},{6,10},{8,12},{10,14},{12,16},{14,18},{16,20},{1... | collective-permute-start | bytes 3145736 | tf_op jit(solution)/shard_map/ppermute | solution.py:141
  33.7 47.8 %collective-permute-start.1 = (bf16[512,1024]{1,0:T(8,128)(2,1)}, bf16[512,1024]{1,0:T(8,128)(2,1)}, u32[]{:S(2)}, u32[]{:S(2)}) collective-permute-start(bf16[512,1024]{1,0:T(8,128)(2,1)} %add_convert_fusion.1), channel_id=1, source_target_pairs={{0,2},{2,4},{4,6},{6,8},{8,10},{10,12},{12,14},{14,16},{16,18},{18... | collective-permute-start | bytes 3145736 | tf_op jit(solution)/shard_map/ppermute | solution.py:141
  45.0 3.9 copy-start.1
  45.0 3.9 copy-start.20
  201.4 6.0 %copy-start.4 = (pred[512,1536]{0,1:T(8,128)(4,1)}, pred[512,1536]{0,1:T(8,128)(4,1)S(1)}, u32[]{:S(2)}) copy-start(pred[512,1536]{0,1:T(8,128)(4,1)S(1)} %fusion.136) | copy-start | bytes 2359300 | tf_op jit(solution)/shard_map/while
  202.1 5.3 %copy-start.13 = (f32[2,512]{1,0:T(2,128)}, f32[2,512]{1,0:T(2,128)S(1)}, u32[]{:S(2)}) copy-start(f32[2,512]{1,0:T(2,128)S(1)} %dynamic-slice_bitcast_fusion.2) | copy-start | bytes 12292 | tf_op jit(solution)/shard_map/while
  225.4 6.0 %copy-start.4 = (pred[512,1536]{0,1:T(8,128)(4,1)}, pred[512,1536]{0,1:T(8,128)(4,1)S(1)}, u32[]{:S(2)}) copy-start(pred[512,1536]{0,1:T(8,128)(4,1)S(1)} %fusion.136) | copy-start | bytes 2359300 | tf_op jit(solution)/shard_map/while
  226.2 5.3 %copy-start.13 = (f32[2,512]{1,0:T(2,128)}, f32[2,512]{1,0:T(2,128)S(1)}, u32[]{:S(2)}) copy-start(f32[2,512]{1,0:T(2,128)S(1)} %dynamic-slice_bitcast_fusion.2) | copy-start | bytes 12292 | tf_op jit(solution)/shard_map/while
  249.5 6.0 %copy-start.4 = (pred[512,1536]{0,1:T(8,128)(4,1)}, pred[512,1536]{0,1:T(8,128)(4,1)S(1)}, u32[]{:S(2)}) copy-start(pred[512,1536]{0,1:T(8,128)(4,1)S(1)} %fusion.136) | copy-start | bytes 2359300 | tf_op jit(solution)/shard_map/while
  250.2 5.3 %copy-start.13 = (f32[2,512]{1,0:T(2,128)}, f32[2,512]{1,0:T(2,128)S(1)}, u32[]{:S(2)}) copy-start(f32[2,512]{1,0:T(2,128)S(1)} %dynamic-slice_bitcast_fusion.2) | copy-start | bytes 12292 | tf_op jit(solution)/shard_map/while
  273.5 6.0 %copy-start.4 = (pred[512,1536]{0,1:T(8,128)(4,1)}, pred[512,1536]{0,1:T(8,128)(4,1)S(1)}, u32[]{:S(2)}) copy-start(pred[512,1536]{0,1:T(8,128)(4,1)S(1)} %fusion.136) | copy-start | bytes 2359300 | tf_op jit(solution)/shard_map/while
  274.2 5.2 %copy-start.13 = (f32[2,512]{1,0:T(2,128)}, f32[2,512]{1,0:T(2,128)S(1)}, u32[]{:S(2)}) copy-start(f32[2,512]{1,0:T(2,128)S(1)} %dynamic-slice_bitcast_fusion.2) | copy-start | bytes 12292 | tf_op jit(solution)/shard_map/while
  297.5 6.0 %copy-start.4 = (pred[512,1536]{0,1:T(8,128)(4,1)}, pred[512,1536]{0,1:T(8,128)(4,1)S(1)}, u32[]{:S(2)}) copy-start(pred[512,1536]{0,1:T(8,128)(4,1)S(1)} %fusion.136) | copy-start | bytes 2359300 | tf_op jit(solution)/shard_map/while
  298.2 5.3 %copy-start.13 = (f32[2,512]{1,0:T(2,128)}, f32[2,512]{1,0:T(2,128)S(1)}, u32[]{:S(2)}) copy-start(f32[2,512]{1,0:T(2,128)S(1)} %dynamic-slice_bitcast_fusion.2) | copy-start | bytes 12292 | tf_op jit(solution)/shard_map/while
  321.5 6.0 %copy-start.4 = (pred[512,1536]{0,1:T(8,128)(4,1)}, pred[512,1536]{0,1:T(8,128)(4,1)S(1)}, u32[]{:S(2)}) copy-start(pred[512,1536]{0,1:T(8,128)(4,1)S(1)} %fusion.136) | copy-start | bytes 2359300 | tf_op jit(solution)/shard_map/while
  322.3 5.3 %copy-start.13 = (f32[2,512]{1,0:T(2,128)}, f32[2,512]{1,0:T(2,128)S(1)}, u32[]{:S(2)}) copy-start(f32[2,512]{1,0:T(2,128)S(1)} %dynamic-slice_bitcast_fusion.2) | copy-start | bytes 12292 | tf_op jit(solution)/shard_map/while
  345.5 6.0 %copy-start.4 = (pred[512,1536]{0,1:T(8,128)(4,1)}, pred[512,1536]{0,1:T(8,128)(4,1)S(1)}, u32[]{:S(2)}) copy-start(pred[512,1536]{0,1:T(8,128)(4,1)S(1)} %fusion.136) | copy-start | bytes 2359300 | tf_op jit(solution)/shard_map/while
  346.3 5.2 %copy-start.13 = (f32[2,512]{1,0:T(2,128)}, f32[2,512]{1,0:T(2,128)S(1)}, u32[]{:S(2)}) copy-start(f32[2,512]{1,0:T(2,128)S(1)} %dynamic-slice_bitcast_fusion.2) | copy-start | bytes 12292 | tf_op jit(solution)/shard_map/while
  369.5 6.0 %copy-start.4 = (pred[512,1536]{0,1:T(8,128)(4,1)}, pred[512,1536]{0,1:T(8,128)(4,1)S(1)}, u32[]{:S(2)}) copy-start(pred[512,1536]{0,1:T(8,128)(4,1)S(1)} %fusion.136) | copy-start | bytes 2359300 | tf_op jit(solution)/shard_map/while
  370.3 5.3 %copy-start.13 = (f32[2,512]{1,0:T(2,128)}, f32[2,512]{1,0:T(2,128)S(1)}, u32[]{:S(2)}) copy-start(f32[2,512]{1,0:T(2,128)S(1)} %dynamic-slice_bitcast_fusion.2) | copy-start | bytes 12292 | tf_op jit(solution)/shard_map/while
  389.5 8.3 %copy-start.3 = (f32[512,2048]{0,1:T(8,128)S(1)}, f32[512,2048]{0,1:T(8,128)}, u32[]{:S(2)}) copy-start(f32[512,2048]{0,1:T(8,128)} %get-tuple-element.431) | copy-start | bytes 12582916
  394.6 49.1 %collective-permute-start.4 = (f32[512,1024]{1,0:T(8,128)}, f32[512,1024]{1,0:T(8,128)}, u32[]{:S(2)}, u32[]{:S(2)}) collective-permute-start(f32[512,1024]{1,0:T(8,128)} %get-tuple-element.633), channel_id=1, source_target_pairs={{2,0},{4,2},{6,4},{8,6},{10,8},{12,10},{14,12},{16,14},{18,16},{20... | collective-permute-start | bytes 6291464 | tf_op jit(solution)/shard_map/ppermute | solution.py:141
  396.5 51.1 %collective-permute-start.5 = (f32[512,1024]{1,0:T(8,128)}, f32[512,1024]{1,0:T(8,128)}, u32[]{:S(2)}, u32[]{:S(2)}) collective-permute-start(f32[512,1024]{1,0:T(8,128)} %get-tuple-element.634), channel_id=1, source_target_pairs={{4,0},{6,2},{8,4},{10,6},{12,8},{14,10},{16,12},{18,14},{20,16},{2... | collective-permute-start | bytes 6291464 | tf_op jit(solution)/shard_map/ppermute | solution.py:141
  409.9 4.9 copy-start.8
  414.8 4.8 copy-start.2
  414.8 5.9 %copy-start.5 = (f32[512,2048]{1,0:T(8,128)S(1)}, f32[512,2048]{1,0:T(8,128)}, u32[]{:S(2)}) copy-start(f32[512,2048]{1,0:T(8,128)} %copy.55) | copy-start | bytes 12582916
  420.7 4.5 copy-start.19
  420.7 4.9 copy-start.10
  426.3 24.7 %copy-start.12 = (bf16[16,1024]{1,0:T(8,128)(2,1)S(1)}, bf16[16,1024]{1,0:T(8,128)(2,1)}, u32[]{:S(2)}) copy-start(bf16[16,1024]{1,0:T(8,128)(2,1)} %param.22) | copy-start | bytes 98308
  426.3 25.1 %copy-start.17 = (bf16[512,16]{0,1:T(8,128)(2,1)S(1)}, bf16[512,16]{0,1:T(8,128)(2,1)}, u32[]{:S(2)}) copy-start(bf16[512,16]{0,1:T(8,128)(2,1)} %copy-done.16) | copy-start | bytes 49156

commit v2 on v1

v2 whole, which is shorter than its diff:
```python
import functools
import math

import jax
import jax.numpy as jnp
import numpy as np
from jax import lax
from jax.experimental import pallas as pl
from jax.experimental.pallas import tpu as pltpu
from jax.sharding import PartitionSpec as P

D = 5376
QUERY_HEADS = 32
KEY_VALUE_HEADS = 16
HEAD_SIZE = 128
WINDOW = 1024
BLOCK = 128
ROPE_BASE = 10000.0

TOKENS = 512
FEATURES = 2688
KV = 8
PAIR = 2 * HEAD_SIZE
ROWS = 256
SPAN = WINDOW + ROWS
REACH = WINDOW + TOKENS
AHEAD = 3
LAG = 2
HIDDEN = -1e30
SCALE = (D // QUERY_HEADS) ** -0.5
BF16 = jnp.bfloat16
F32 = jnp.float32

RANK = 16
GROUP = 8
CHUNK = 1152
MESH = pl.DeviceIdType.MESH


def pieces_of(widths):
    pieces, start = [], 0
    for which, width in enumerate(widths):
        done = 0
        while done < width:
            chunk, inside = divmod(start + done, CHUNK)
            count = min(width - done, CHUNK - inside)
            pieces.append((which, done, chunk, inside, count))
            done += count
        start += width
    return pieces


def total_kernel(
    widths,
    scale,
    parts,
    o_0,
    o_1,
    o_2,
    o_3,
    near,
    far,
    final,
    near_send,
    near_recv,
    far_send,
    far_recv,
    final_send,
    final_recv,
):
    ctx, head = lax.axis_index("ctx"), lax.axis_index("head")
    member = ctx % GROUP
    group = ctx // GROUP
    near_peers = [group * GROUP + (member + by) % GROUP for by in range(1, GROUP)]
    far_peers = [((group + by) % GROUP) * GROUP + member for by in range(1, GROUP)]

    barrier = pltpu.get_barrier_semaphore()
    for peer in near_peers + far_peers:
        pl.semaphore_signal(barrier, inc=1, device_id=(peer, head), device_id_type=MESH)
    pl.semaphore_wait(barrier, 2 * (GROUP - 1))

    def copy(source, target, send, recv, peer):
        return pltpu.make_async_remote_copy(
            src_ref=source,
            dst_ref=target,
            send_sem=send,
            recv_sem=recv,
            device_id=(peer, head),
            device_id_type=MESH,
        )

    copies = []
    for k, peer in enumerate(near_peers):
        one = copy(
            parts.at[peer % GROUP], near.at[k], near_send.at[k], near_recv.at[k], peer
        )
        one.start()
        copies.append(one)
    total = parts[member].astype(jnp.float32)
    for k, one in enumerate(copies):
        one.wait_recv()
        total += near[k].astype(jnp.float32)
    far[group] = total.astype(jnp.bfloat16)

    far_copies = []
    for k, peer in enumerate(far_peers):
        one = copy(far.at[group], far.at[group], far_send.at[k], far_recv.at[k], peer)
        one.start()
        far_copies.append(one)
    for one in far_copies:
        one.wait_recv()
    total = far[0].astype(jnp.float32)
    for k in range(1, GROUP):
        total += far[k].astype(jnp.float32)
    final[member] = (total * scale).astype(jnp.bfloat16)

    last_copies = []
    for k, peer in enumerate(near_peers):
        one = copy(final.at[member], final.at[member], final_send.at[k], final_recv.at[k], peer)
        one.start()
        last_copies.append(one)
    for one in last_copies:
        one.wait_recv()
    outs = (o_0, o_1, o_2, o_3)
    for which, at, chunk, inside, count in pieces_of(widths):
        outs[which][:, at : at + count] = final[chunk, :, inside : inside + count].astype(
            jnp.float32
        )
    for one in copies + far_copies + last_copies:
        one.wait_send()


def total_over_ctx(parts, widths, scale):
    chunked = (GROUP, RANK, CHUNK)
    return pl.pallas_call(
        functools.partial(total_kernel, widths, scale),
        out_shape=[jax.ShapeDtypeStruct((RANK, width), jnp.float32) for width in widths],
        in_specs=[pl.BlockSpec(memory_space=pltpu.VMEM)],
        out_specs=[pl.BlockSpec(memory_space=pltpu.VMEM)] * len(widths),
        scratch_shapes=[
            pltpu.VMEM((GROUP - 1, RANK, CHUNK), jnp.bfloat16),
            pltpu.VMEM(chunked, jnp.bfloat16),
            pltpu.VMEM(chunked, jnp.bfloat16),
        ]
        + [pltpu.SemaphoreType.DMA((GROUP - 1,))] * 6,
        compiler_params=pltpu.CompilerParams(
            collective_id=0, has_side_effects=True, vmem_limit_bytes=24 * 2**20
        ),
    )(parts)


def turns_of_angles():
    half = HEAD_SIZE // 2
    turns = ROPE_BASE ** (-2.0 * np.arange(half) / HEAD_SIZE) / (2.0 * math.pi)
    mantissa, exponent = np.frexp(turns)
    coarse = np.ldexp(np.floor(mantissa * 256.0), exponent - 8)
    rows = np.stack([np.tile(coarse, 2), np.tile(turns - coarse, 2)])
    return np.concatenate([rows, np.zeros((6, HEAD_SIZE))]).astype(np.float32)


def nearest(x):
    return jnp.floor(x + 0.5)


def sine_of_turns(r):
    r = r - nearest(r)
    r = jnp.where(r > 0.25, 0.5 - r, jnp.where(r < -0.25, -0.5 - r, r))
    x = r * (2.0 * math.pi)
    y = x * x
    out = jnp.full_like(y, -1.0 / math.factorial(11))
    for power in (9, 7, 5, 3, 1):
        sign = 1.0 if power % 4 == 1 else -1.0
        out = out * y + sign / math.factorial(power)
    return out * x


def dot(a, b, contract):
    return lax.dot_general(a, b, ((contract[:1], contract[1:]), ((), ())), preferred_element_type=F32)


def layer_kernel(
    hidden_hbm,
    query_hbm,
    key_hbm,
    value_hbm,
    query_down_hbm,
    query_up_hbm,
    value_down_hbm,
    value_up_hbm,
    positions_ref,
    turns_ref,
    mask_ref,
    gradient_hbm,
    out_hbm,
    parts_ref,
    hidden,
    query_base,
    key_base,
    value_base,
    downs,
    query_up,
    value_up,
    gradient,
    keys,
    values,
    out,
    bias,
    cosines,
    sines,
    low_mine,
    low_theirs,
    low_rows,
    low_cols,
    back_mine,
    back_theirs,
    query_grad,
    value_sum,
    value_own,
    value_sent,
    value_got,
    row,
    load_sem,
    out_sem,
    low_sem,
    back_sem,
    far_send,
    far_recv,
    near_send,
    near_recv,
    grad_send,
    grad_recv,
):
    ctx, head = lax.axis_index("ctx"), lax.axis_index("head")
    count = lax.axis_size("ctx")
    core = ctx % 2
    ahead_1, ahead_2 = (ctx + 1) % count, (ctx + 2) % count
    behind_1, behind_2 = (ctx + count - 1) % count, (ctx + count - 2) % count

    def remote(source, target, send, recv, at_ctx, at_head=head):
        return pltpu.make_async_remote_copy(
            src_ref=source,
            dst_ref=target,
            send_sem=send,
            recv_sem=recv,
            device_id=(at_ctx, at_head),
            device_id_type=MESH,
        )

    loads = [
        pltpu.make_async_copy(source, target, load_sem.at[k])
        for k, (source, target) in enumerate(
            (
                (key_hbm, key_base),
                (query_down_hbm, downs.at[0:RANK]),
                (value_down_hbm, downs.at[RANK : 2 * RANK]),
                (hidden_hbm, hidden),
                (value_up_hbm, value_up.at[RANK : 2 * RANK]),
                (value_hbm, value_base),
                (query_up_hbm, query_up.at[0:RANK]),
                (query_hbm, query_base),
                (gradient_hbm, gradient),
            )
        )
    ]
    for one in loads:
        one.start()

    barrier = pltpu.get_barrier_semaphore()
    for at in ((ahead_1, head), (ahead_2, head), (behind_1, head), (behind_2, head), (ctx, 1 - head)):
        pl.semaphore_signal(barrier, inc=1, device_id=at, device_id_type=MESH)

    lane = lax.broadcasted_iota(jnp.int32, (TOKENS, HEAD_SIZE), 1)
    first_half = lane < HEAD_SIZE // 2
    position = jnp.transpose(
        jnp.broadcast_to(positions_ref[...].astype(F32), (HEAD_SIZE, TOKENS))
    )
    coarse = position * turns_ref[0:1, :]
    fine = position * turns_ref[1:2, :]
    turns = (coarse - nearest(coarse)) + (fine - nearest(fine))
    table = sine_of_turns(turns + jnp.where(first_half, 0.25, 0.0))
    swapped = pltpu.roll(table, HEAD_SIZE // 2, 1)
    cosines[...] = jnp.where(first_half, table, swapped)
    sines[...] = jnp.where(first_half, -swapped, table)

    def rope(x, cos, sin):
        return x * cos + pltpu.roll(x, HEAD_SIZE // 2, 1) * sin

    loads[0].wait()
    for h in range(KV):
        columns = slice(h * HEAD_SIZE, (h + 1) * HEAD_SIZE)
        keys[h, WINDOW:REACH] = rope(
            key_base[:, columns].astype(F32), cosines[...], sines[...]
        ).astype(BF16)

    pl.semaphore_wait(barrier, 5)

    def far_copy(store, kind, h):
        return remote(
            store.at[h, WINDOW:REACH],
            store.at[h, 0:TOKENS],
            far_send.at[kind, h],
            far_recv.at[kind, h],
            ahead_2,
        )

    def near_copy(store, kind, h, first, at_ctx):
        return remote(
            store.at[h, pl.ds(first, TOKENS)],
            store.at[h, TOKENS:WINDOW],
            near_send.at[kind, h],
            near_recv.at[kind, h],
            at_ctx,
        )

    def send_own(store, kind, h):
        far_copy(store, kind, h).start()

        @pl.when(core == 0)
        def _():
            near_copy(store, kind, h, WINDOW, ahead_1).start()

    for h in range(AHEAD):
        send_own(keys, 0, h)

    for one in loads[1:4]:
        one.wait()
    low_mine[...] = dot(downs[...], hidden[...], (1, 1))
    low_copy = remote(low_mine, low_theirs, low_sem.at[0], low_sem.at[1], ctx, 1 - head)
    low_copy.start()

    key_at = lax.broadcasted_iota(jnp.int32, (BLOCK, BLOCK), 1)
    query_at = lax.broadcasted_iota(jnp.int32, (BLOCK, BLOCK), 0)
    for half in range(TOKENS // ROWS):
        for r in range(ROWS // BLOCK):
            block = ctx * (TOKENS // BLOCK) + half * (ROWS // BLOCK) + r
            for j in range(SPAN // BLOCK):
                offset = WINDOW // BLOCK + r - j
                if 0 <= offset <= WINDOW // BLOCK:
                    seen = (mask_ref[offset, block] == 1) & (block >= offset)
                    tile = jnp.full((BLOCK, BLOCK), jnp.where(seen, 0.0, HIDDEN))
                    if offset == 0:
                        tile = jnp.where(key_at <= query_at, tile, HIDDEN)
                    if offset == WINDOW // BLOCK:
                        tile = jnp.where(key_at > query_at, tile, HIDDEN)
                else:
                    tile = jnp.full((BLOCK, BLOCK), HIDDEN, F32)
                bias[
                    half, r * BLOCK : (r + 1) * BLOCK, j * BLOCK : (j + 1) * BLOCK
                ] = tile

    query_up[RANK : 2 * RANK] = jnp.zeros((RANK, KV * PAIR), BF16)
    value_up[0:RANK] = jnp.zeros((RANK, KV * HEAD_SIZE), BF16)
    back_mine[...] = jnp.zeros_like(back_mine)
    row[...] = jnp.zeros_like(row)

    low_copy.wait_recv()
    low = low_mine[...] + low_theirs[...]
    low_rows[...] = low.astype(BF16)
    low_cols[...] = jnp.transpose(low).astype(BF16)
    loads[4].wait()
    loads[5].wait()
    for h in range(KV):
        columns = slice(h * HEAD_SIZE, (h + 1) * HEAD_SIZE)
        values[h, WINDOW:REACH] = (
            value_base[:, columns].astype(F32) + dot(low_cols[...], value_up[:, columns], (1, 0))
        ).astype(BF16)
        if h < AHEAD:
            send_own(values, 1, h)
    for one in loads[6:]:
        one.wait()

    widths = (FEATURES, KV * PAIR, FEATURES, KV * HEAD_SIZE)

    def out_copy(h):
        columns = pl.ds(pl.multiple_of(h * PAIR, PAIR), PAIR)
        return pltpu.make_async_copy(out.at[:, columns], out_hbm.at[:, columns], out_sem.at[h])

    def grad_copy(kind, h):
        return remote(
            value_sent.at[h, kind],
            value_got.at[h, kind],
            grad_send.at[kind, h],
            grad_recv.at[kind, h],
            behind_1 if kind == 0 else behind_2,
        )

    def half_of(h, half):
        rows = slice(half * ROWS, (half + 1) * ROWS)
        span = slice(half * ROWS, half * ROWS + SPAN)
        pair = pl.ds(pl.multiple_of(h * PAIR, PAIR), PAIR)
        cos, sin = cosines[rows], sines[rows]

        def stack(x):
            return jnp.concatenate([x[:, :HEAD_SIZE], x[:, HEAD_SIZE:]], axis=0)

        cos_2 = jnp.concatenate([cos, cos], axis=0)
        sin_2 = jnp.concatenate([sin, sin], axis=0)
        raw = query_base[rows, pair].astype(F32) + dot(
            low_cols[rows], query_up[:, pair], (1, 0)
        )
        queries = (rope(stack(raw), cos_2, sin_2) * (SCALE * math.log2(math.e))).astype(BF16)
        head_keys, head_values = keys[h, span], values[h, span]
        scores = dot(queries, head_keys, (1, 1))
        scores = (
            scores.reshape(2, ROWS, SPAN) + bias[half][None]
        ).reshape(2 * ROWS, SPAN)
        top = jnp.max(scores, axis=1, keepdims=True)
        weights = jnp.exp2(scores - top)
        inverse = 1.0 / jnp.sum(weights, axis=1, keepdims=True)
        rounded = weights.astype(BF16)
        result = (dot(rounded, head_values, (1, 0)) * inverse).astype(BF16)
        out[rows, pair] = jnp.concatenate([result[:ROWS], result[ROWS:]], axis=1)
        scaled = stack(gradient[rows, pair]).astype(F32) * inverse
        delta = jnp.sum(scaled * result.astype(F32), axis=1, keepdims=True)
        scaled = scaled.astype(BF16)
        grad_weights = dot(scaled, head_values, (1, 1))
        grad_scores = (weights * (grad_weights - delta)).astype(BF16)
        turned = rope(dot(grad_scores, head_keys, (1, 0)) * SCALE, cos_2, -sin_2).astype(BF16)
        query_grad[rows] = jnp.concatenate([turned[:ROWS], turned[ROWS:]], axis=1)
        terms = dot(scaled, rounded, (0, 0))
        if half == 0:
            value_sum[:, 0:SPAN] = terms
        else:
            value_sum[:, ROWS:SPAN] += terms[:, : SPAN - ROWS]
            value_sum[:, SPAN:REACH] = terms[:, SPAN - ROWS :]

    def absorb(h):
        grad_copy(0, h).wait_recv()
        grad_copy(1, h).wait_recv()
        total = (
            value_own[h] + value_got[h, 0].astype(F32) + value_got[h, 1].astype(F32)
        ).astype(BF16)
        columns = pl.ds(pl.multiple_of(h * HEAD_SIZE, HEAD_SIZE), HEAD_SIZE)
        back_mine[RANK : 2 * RANK] += dot(value_up[RANK : 2 * RANK, columns], total, (1, 0))
        row[:, pl.ds(pl.multiple_of(h * HEAD_SIZE, HEAD_SIZE) + sum(widths[:3]), HEAD_SIZE)] = dot(
            low_rows[RANK : 2 * RANK], total, (1, 1)
        )

    def one_head(h, carry):
        far_copy(keys, 0, h).wait_recv()
        far_copy(values, 1, h).wait_recv()

        @pl.when(core == 1)
        def _():
            near_copy(keys, 0, h, 0, behind_1).start()
            near_copy(values, 1, h, 0, behind_1).start()

        @pl.when(h + AHEAD < KV)
        def _():
            send_own(keys, 0, h + AHEAD)
            send_own(values, 1, h + AHEAD)

        near_copy(keys, 0, h, 0, behind_1).wait_recv()
        near_copy(values, 1, h, 0, behind_1).wait_recv()
        half_of(h, 0)
        half_of(h, 1)
        value_sent[h, 1] = value_sum[:, 0:TOKENS].astype(BF16)
        value_sent[h, 0] = value_sum[:, TOKENS:WINDOW].astype(BF16)
        grad_copy(1, h).start()
        grad_copy(0, h).start()
        value_own[h] = value_sum[:, WINDOW:REACH]
        out_copy(h).start()
        pair = pl.ds(pl.multiple_of(h * PAIR, PAIR), PAIR)
        back_mine[0:RANK] += dot(query_up[0:RANK, pair], query_grad[...], (1, 1))
        row[:, pl.ds(pl.multiple_of(h * PAIR, PAIR) + widths[0], PAIR)] = dot(
            low_rows[0:RANK], query_grad[...], (1, 0)
        )

        @pl.when(h >= LAG)
        def _():
            absorb(h - LAG)

        return carry

    lax.fori_loop(0, KV, one_head, 0)
    for h in range(KV - LAG, KV):
        absorb(h)

    back_copy = remote(back_mine, back_theirs, back_sem.at[0], back_sem.at[1], ctx, 1 - head)
    back_copy.start()
    back_copy.wait_recv()
    back = (back_mine[...] + back_theirs[...]).astype(BF16)
    down = dot(back, hidden[...], (1, 0))
    row[:, 0:FEATURES] = down[0:RANK]
    start = widths[0] + widths[1]
    row[:, start : start + FEATURES] = down[RANK:]
    for k in range(GROUP):
        parts_ref[k] = row[:, k * CHUNK : (k + 1) * CHUNK].astype(BF16)

    low_copy.wait_send()
    back_copy.wait_send()

    def finish(h, carry):
        for kind, store in ((0, keys), (1, values)):
            far_copy(store, kind, h).wait_send()
            near_copy(store, kind, h, 0, behind_1).wait_send()
            grad_copy(kind, h).wait_send()
        out_copy(h).wait()
        return carry

    lax.fori_loop(0, KV, finish, 0)


def per_device(
    hidden_states,
    query_base,
    key_base,
    frozen_value_rows,
    query_down,
    query_up,
    value_down,
    value_up_weight,
    positions,
    block_mask,
    output_gradient,
):
    anywhere = pl.BlockSpec(memory_space=pl.ANY)
    in_vmem = pl.BlockSpec(memory_space=pltpu.VMEM)
    columns = KV * HEAD_SIZE
    head_store = pltpu.VMEM((KV, REACH, HEAD_SIZE), BF16)
    value_terms = pltpu.VMEM((KV, 2, HEAD_SIZE, TOKENS), BF16)
    low_shape = pltpu.VMEM((2 * RANK, TOKENS), F32)
    dma = pltpu.SemaphoreType.DMA
    attention_out, parts = pl.pallas_call(
        layer_kernel,
        out_shape=[
            jax.ShapeDtypeStruct((TOKENS, 2 * columns), BF16),
            jax.ShapeDtypeStruct((GROUP, RANK, CHUNK), BF16),
        ],
        in_specs=[anywhere] * 8
        + [in_vmem, in_vmem, pl.BlockSpec(memory_space=pltpu.SMEM), anywhere],
        out_specs=[anywhere, in_vmem],
        scratch_shapes=[
            pltpu.VMEM((TOKENS, FEATURES), BF16),
            pltpu.VMEM((TOKENS, 2 * columns), BF16),
            pltpu.VMEM((TOKENS, columns), BF16),
            pltpu.VMEM((TOKENS, columns), BF16),
            pltpu.VMEM((2 * RANK, FEATURES), BF16),
            pltpu.VMEM((2 * RANK, 2 * columns), BF16),
            pltpu.VMEM((2 * RANK, columns), BF16),
            pltpu.VMEM((TOKENS, 2 * columns), BF16),
            head_store,
            head_store,
            pltpu.VMEM((TOKENS, 2 * columns), BF16),
            pltpu.VMEM((TOKENS // ROWS, ROWS, SPAN), F32),
            pltpu.VMEM((TOKENS, HEAD_SIZE), F32),
            pltpu.VMEM((TOKENS, HEAD_SIZE), F32),
            low_shape,
            low_shape,
            pltpu.VMEM((2 * RANK, TOKENS), BF16),
            pltpu.VMEM((TOKENS, 2 * RANK), BF16),
            low_shape,
            low_shape,
            pltpu.VMEM((TOKENS, PAIR), BF16),
            pltpu.VMEM((HEAD_SIZE, REACH), F32),
            pltpu.VMEM((KV, HEAD_SIZE, TOKENS), F32),
            value_terms,
            value_terms,
            pltpu.VMEM((RANK, GROUP * CHUNK), F32),
            dma((9,)),
            dma((KV,)),
            dma((2,)),
            dma((2,)),
        ]
        + [dma((2, KV))] * 6,
        compiler_params=pltpu.CompilerParams(
            collective_id=1, has_side_effects=True, vmem_limit_bytes=56 * 2**20
        ),
    )(
        hidden_states,
        query_base,
        key_base,
        frozen_value_rows,
        query_down.T,
        query_up,
        value_down.T,
        value_up_weight,
        positions.reshape(1, TOKENS),
        turns_of_angles(),
        block_mask.T,
        output_gradient,
    )
    widths = (FEATURES, 2 * columns, FEATURES, columns)
    tokens_all = TOKENS * lax.axis_size("ctx")
    down_query, up_query, down_value, up_value = total_over_ctx(
        parts, widths, tokens_all**-0.5
    )
    return attention_out, down_query.T, up_query, down_value.T, up_value


def solution(mesh):
    placed = (
        P("ctx", "head"),
        P("ctx", "head"),
        P("ctx", "head"),
        P("ctx", "head"),
        P("head", None),
        P(None, "head"),
        P("head", None),
        P(None, "head"),
        P("ctx"),
        P(),
        P("ctx", "head"),
    )
    return jax.shard_map(
        per_device,
        mesh=mesh,
        in_specs=placed,
        out_specs=(
            P("ctx", "head"),
            P("head", None),
            P(None, "head"),
            P("head", None),
            P(None, "head"),
        ),
        check_vma=False,
    )
```

time: 523 us -> 116 us (0.22); the launches traced: 514 us -> 116 us
  matrix products: 177 us -> 0 us
  other arithmetic: 110 us -> 0 us
  local copies, waits for them, and re-layouts: 95.3 us -> 6.73 us
  Pallas kernels: 51.3 us -> 108 us
  waiting for transfers between devices: 45.2 us -> 0 us
  starting transfers between devices: 18.9 us -> 0 us
  blocking collectives: 14.5 us -> 0 us
    dot_general x50 -> x0, matrix products: 177 us -> none  [the longest x16 55.1 us: head_scores(): jnp.einsum('lgd,kd->glk', head_queries, head_keys, preferred_element_type...]
    pallas_call x0 -> x1, Pallas kernels: none -> 81.8 us  [per_device(): pl.pallas_call(layer_kernel, out_shape=[jax.ShapeDtypeStruct((TOKENS, 2 *...]
    ppermute x6 -> x0, waiting for transfers between devices: 45.2 us -> none  [shifted(): return lax.ppermute(x, axis, pairs)]
    and x16 -> x0, other arithmetic: 38.6 us -> none  [allowed_pairs(): return token_ok & spread_out]
    pallas_call x1, Pallas kernels: 51.3 us -> 26.4 us  [total_over_ctx(): pl.pallas_call(functools.partial(total_kernel, widths, scale), out_shape=...]
    reduce_sum x16 -> x0, other arithmetic: 24.5 us -> none  [the longest x8 13 us: backward_one_head(): jnp.sum(head_grads.astype(jnp.float32) * head_outs.astype(jnp.float32), a...]
    dynamic_slice x32 -> x0, local copies, waits for them, and re-layouts: 24.3 us -> none  [the longest x16 15.5 us: head_scores(): lax.dynamic_slice_in_dim(query_rows, head_index * query_groups * HEAD_SIZ...]
    ppermute x6 -> x0, starting transfers between devices: 18.9 us -> none  [shifted(): return lax.ppermute(x, axis, pairs)]
  transfers between devices with their start and end apart: 6 -> 0, of which waited for: 5 -> 0; matrix products, arithmetic and copies ran while one was open for 10% -> 0% of each run, Pallas kernels for 0% -> 0%
where the time goes in v2:
time: 116 us
  Pallas kernels  108 us (93%)
  local copies, waits for them, and re-layouts  6.73 us (6%)
    pallas_call x1, Pallas kernels, per_device(): pl.pallas_call(layer_kernel, out_shape=[jax.ShapeDtypeStruct((TOKENS, 2 *...  81.8 us
    pallas_call x1, Pallas kernels, total_over_ctx(): pl.pallas_call(functools.partial(total_kernel, widths, scale), out_shape=...  26.4 us
    unnamed x7, local copies, waits for them, and re-layouts  6.73 us

profile of v2, /device:TPU:1, one launch (start us, length us, event | category | flops | bytes accessed | tf_op | source)
XLA Modules:
  0.0 115.6 jit_solution(7675409735366723685)
XLA Ops:
  0.6 81.8 %shard_map.155 = (bf16[512,2048]{1,0:T(8,128)(2,1)}, bf16[8,16,1152]{2,1,0:T(8,128)(2,1)}) custom-call(bf16[512,2688]{1,0:T(8,128)(2,1)} %hidden_hbm.1, bf16[512,2048]{1,0:T(8,128)(2,1)} %query_hbm.1, bf16[512,1024]{1,0:T(8,128)(2,1)} %key_hbm.1, bf16[512,1024]{1,0:T(8,128)(2,1)} %value_hbm.1, bf16[16,2688]{1,0:T(8,128)(2,1)} %bitcast.8, ...), custom_call_target="tpu_custom_call" | custom-call | tf_op jit(solution)/shard_map/pallas_call | solution.py:524
  82.4 0.0 copy-start
  82.4 1.0 copy-done
  83.4 26.4 %shard_map.156 = (f32[16,2688]{1,0:T(8,128)S(1)}, f32[16,2048]{1,0:T(8,128)S(1)}, f32[16,2688]{1,0:T(8,128)S(1)}, f32[16,1024]{1,0:T(8,128)S(1)}) custom-call(bf16[8,16,1152]{2,1,0:T(8,128)(2,1)S(1)} %copy-done), custom_call_target="tpu_custom_call" | custom-call | tf_op jit(solution)/shard_map/pallas_call | solution.py:135
  109.8 3.2 %copy.22 = bf16[512,2048]{1,0:T(8,128)(2,1)} copy(bf16[512,2048]{1,0:T(8,128)(2,1)} %get-tuple-element.22) | data formatting | bytes 4194304
  112.9 0.7 copy.23
  113.6 0.7 copy.24
  114.3 0.7 copy.25
  114.9 0.6 copy.26
Async XLA Ops:
  82.4 1.0 copy-start

commit v3 on v2

v3 whole, which is shorter than its diff:
```python
import functools
import math

import jax
import jax.numpy as jnp
import numpy as np
from jax import lax
from jax.experimental import pallas as pl
from jax.experimental.pallas import tpu as pltpu
from jax.sharding import PartitionSpec as P

D = 5376
QUERY_HEADS = 32
KEY_VALUE_HEADS = 16
HEAD_SIZE = 128
WINDOW = 1024
BLOCK = 128
ROPE_BASE = 10000.0

TOKENS = 512
FEATURES = 2688
KV = 8
PAIR = 2 * HEAD_SIZE
ROWS = 256
SPAN = WINDOW + ROWS
REACH = WINDOW + TOKENS
AHEAD = 4
LAG = 3
HIDDEN = -1e30
SCALE = (D // QUERY_HEADS) ** -0.5
BF16 = jnp.bfloat16
F32 = jnp.float32

RANK = 16
GROUP = 8
PIECES = 4
MESH = pl.DeviceIdType.MESH


def pieces_of(widths, chunk_width):
    pieces, start = [], 0
    for which, width in enumerate(widths):
        done = 0
        while done < width:
            chunk, inside = divmod(start + done, chunk_width)
            size = min(width - done, chunk_width - inside)
            pieces.append((which, done, chunk, inside, size))
            done += size
        start += width
    return pieces


def turns_of_angles():
    half = HEAD_SIZE // 2
    turns = ROPE_BASE ** (-2.0 * np.arange(half) / HEAD_SIZE) / (2.0 * math.pi)
    mantissa, exponent = np.frexp(turns)
    coarse = np.ldexp(np.floor(mantissa * 256.0), exponent - 8)
    rows = np.stack([np.tile(coarse, 2), np.tile(turns - coarse, 2)])
    return np.concatenate([rows, np.zeros((6, HEAD_SIZE))]).astype(np.float32)


def nearest(x):
    return jnp.floor(x + 0.5)


def sine_of_turns(r):
    r = r - nearest(r)
    r = jnp.where(r > 0.25, 0.5 - r, jnp.where(r < -0.25, -0.5 - r, r))
    x = r * (2.0 * math.pi)
    y = x * x
    out = jnp.full_like(y, -1.0 / math.factorial(11))
    for power in (9, 7, 5, 3, 1):
        sign = 1.0 if power % 4 == 1 else -1.0
        out = out * y + sign / math.factorial(power)
    return out * x


def dot(a, b, contract):
    return lax.dot_general(a, b, ((contract[:1], contract[1:]), ((), ())), preferred_element_type=F32)


def layer_kernel(
    hidden_hbm,
    query_hbm,
    key_hbm,
    value_hbm,
    query_down_hbm,
    query_up_hbm,
    value_down_hbm,
    value_up_hbm,
    positions_ref,
    turns_ref,
    mask_ref,
    gradient_hbm,
    out_hbm,
    final_query,
    final_value,
    hidden,
    query_base,
    key_base,
    value_base,
    downs,
    query_up,
    value_up,
    gradient,
    keys,
    values,
    out,
    bias,
    cosines,
    sines,
    low_mine,
    low_theirs,
    low_rows,
    low_cols,
    back_mine,
    back_theirs,
    query_grad,
    value_sum,
    value_own,
    value_sent,
    value_got,
    row_query,
    row_value,
    parts_query,
    parts_value,
    near_query,
    near_value,
    away_query,
    away_value,
    load_sem,
    out_sem,
    low_sem,
    back_sem,
    far_send,
    far_recv,
    near_send,
    near_recv,
    grad_send,
    grad_recv,
    sum_send,
    sum_recv,
):
    ctx, head = lax.axis_index("ctx"), lax.axis_index("head")
    count = lax.axis_size("ctx")
    core = ctx % 2
    ahead_1, ahead_2 = (ctx + 1) % count, (ctx + 2) % count
    behind_1, behind_2 = (ctx + count - 1) % count, (ctx + count - 2) % count

    def remote(source, target, send, recv, at_ctx, at_head=head):
        return pltpu.make_async_remote_copy(
            src_ref=source,
            dst_ref=target,
            send_sem=send,
            recv_sem=recv,
            device_id=(at_ctx, at_head),
            device_id_type=MESH,
        )

    loads = [
        pltpu.make_async_copy(source, target, load_sem.at[k])
        for k, (source, target) in enumerate(
            (
                (key_hbm, key_base),
                (query_down_hbm, downs.at[0:RANK]),
                (value_down_hbm, downs.at[RANK : 2 * RANK]),
                (hidden_hbm, hidden),
                (value_up_hbm, value_up.at[RANK : 2 * RANK]),
                (value_hbm, value_base),
                (query_up_hbm, query_up.at[0:RANK]),
                (query_hbm, query_base),
                (gradient_hbm, gradient),
            )
        )
    ]
    for one in loads:
        one.start()

    barrier = pltpu.get_barrier_semaphore()
    member, group = ctx % GROUP, ctx // GROUP
    groups = count // GROUP
    near_peers = [group * GROUP + (member + by) % GROUP for by in range(1, GROUP)]
    far_peers = [((group + by) % groups) * GROUP + member for by in range(1, groups)]
    greeted = [(at, head) for at in (ahead_1, ahead_2, behind_1, behind_2)]
    greeted += [(ctx, 1 - head)] + [(at, head) for at in near_peers + far_peers]
    for at in greeted:
        pl.semaphore_signal(barrier, inc=1, device_id=at, device_id_type=MESH)

    lane = lax.broadcasted_iota(jnp.int32, (TOKENS, HEAD_SIZE), 1)
    first_half = lane < HEAD_SIZE // 2
    position = jnp.transpose(
        jnp.broadcast_to(positions_ref[...].astype(F32), (HEAD_SIZE, TOKENS))
    )
    coarse = position * turns_ref[0:1, :]
    fine = position * turns_ref[1:2, :]
    turns = (coarse - nearest(coarse)) + (fine - nearest(fine))
    table = sine_of_turns(turns + jnp.where(first_half, 0.25, 0.0))
    swapped = pltpu.roll(table, HEAD_SIZE // 2, 1)
    cosines[...] = jnp.where(first_half, table, swapped)
    sines[...] = jnp.where(first_half, -swapped, table)

    def rope(x, cos, sin):
        return x * cos + pltpu.roll(x, HEAD_SIZE // 2, 1) * sin

    loads[0].wait()
    for h in range(KV):
        columns = slice(h * HEAD_SIZE, (h + 1) * HEAD_SIZE)
        keys[h, WINDOW:REACH] = rope(
            key_base[:, columns].astype(F32), cosines[...], sines[...]
        ).astype(BF16)

    pl.semaphore_wait(barrier, len(greeted))

    def far_copy(store, kind, h):
        return remote(
            store.at[h, WINDOW:REACH],
            store.at[h, 0:TOKENS],
            far_send.at[kind, h],
            far_recv.at[kind, h],
            ahead_2,
        )

    def near_copy(store, kind, h, first, at_ctx):
        return remote(
            store.at[h, pl.ds(first, TOKENS)],
            store.at[h, TOKENS:WINDOW],
            near_send.at[kind, h],
            near_recv.at[kind, h],
            at_ctx,
        )

    def send_own(store, kind, h):
        @pl.when(ctx + 2 < count)
        def _():
            far_copy(store, kind, h).start()

        @pl.when(core == 0)
        def _():
            near_copy(store, kind, h, WINDOW, ahead_1).start()

    for h in range(AHEAD):
        send_own(keys, 0, h)

    for one in loads[1:4]:
        one.wait()
    low_mine[...] = dot(downs[...], hidden[...], (1, 1))
    low_copy = remote(low_mine, low_theirs, low_sem.at[0], low_sem.at[1], ctx, 1 - head)
    low_copy.start()

    key_at = lax.broadcasted_iota(jnp.int32, (BLOCK, BLOCK), 1)
    query_at = lax.broadcasted_iota(jnp.int32, (BLOCK, BLOCK), 0)
    for half in range(TOKENS // ROWS):
        for r in range(ROWS // BLOCK):
            block = ctx * (TOKENS // BLOCK) + half * (ROWS // BLOCK) + r
            for j in range(SPAN // BLOCK):
                offset = WINDOW // BLOCK + r - j
                if 0 <= offset <= WINDOW // BLOCK:
                    seen = (mask_ref[offset, block] == 1) & (block >= offset)
                    tile = jnp.full((BLOCK, BLOCK), jnp.where(seen, 0.0, HIDDEN))
                    if offset == 0:
                        tile = jnp.where(key_at <= query_at, tile, HIDDEN)
                    if offset == WINDOW // BLOCK:
                        tile = jnp.where(key_at > query_at, tile, HIDDEN)
                else:
                    tile = jnp.full((BLOCK, BLOCK), HIDDEN, F32)
                bias[
                    half, r * BLOCK : (r + 1) * BLOCK, j * BLOCK : (j + 1) * BLOCK
                ] = tile

    query_up[RANK : 2 * RANK] = jnp.zeros((RANK, KV * PAIR), BF16)
    value_up[0:RANK] = jnp.zeros((RANK, KV * HEAD_SIZE), BF16)
    back_mine[...] = jnp.zeros_like(back_mine)
    for padded, used in ((row_query, FEATURES + KV * PAIR), (row_value, FEATURES + KV * HEAD_SIZE)):
        padded[:, used:] = jnp.zeros((RANK, padded.shape[1] - used), F32)

    @pl.when(ctx < 2)
    def _():
        for store in (keys, values):
            store[:, 0:TOKENS] = jnp.zeros((KV, TOKENS, HEAD_SIZE), BF16)

    @pl.when(ctx < 1)
    def _():
        for store in (keys, values):
            store[:, TOKENS:WINDOW] = jnp.zeros((KV, TOKENS, HEAD_SIZE), BF16)

    @pl.when(ctx + 2 >= count)
    def _():
        value_got[:, 1] = jnp.zeros((KV, HEAD_SIZE, TOKENS), BF16)

    @pl.when(ctx + 1 >= count)
    def _():
        value_got[:, 0] = jnp.zeros((KV, HEAD_SIZE, TOKENS), BF16)

    low_copy.wait_recv()
    low = low_mine[...] + low_theirs[...]
    low_rows[...] = low.astype(BF16)
    low_cols[...] = jnp.transpose(low).astype(BF16)
    loads[4].wait()
    loads[5].wait()
    for h in range(KV):
        columns = slice(h * HEAD_SIZE, (h + 1) * HEAD_SIZE)
        values[h, WINDOW:REACH] = (
            value_base[:, columns].astype(F32) + dot(low_cols[...], value_up[:, columns], (1, 0))
        ).astype(BF16)
        if h < AHEAD:
            send_own(values, 1, h)
    for one in loads[6:]:
        one.wait()

    def out_copy(h):
        columns = pl.ds(pl.multiple_of(h * PAIR, PAIR), PAIR)
        return pltpu.make_async_copy(out.at[:, columns], out_hbm.at[:, columns], out_sem.at[h])

    def grad_copy(kind, h):
        return remote(
            value_sent.at[h, kind],
            value_got.at[h, kind],
            grad_send.at[kind, h],
            grad_recv.at[kind, h],
            behind_1 if kind == 0 else behind_2,
        )

    def stack(x):
        return jnp.concatenate([x[:, :HEAD_SIZE], x[:, HEAD_SIZE:]], axis=0)

    def beside(x):
        return jnp.concatenate([x[:ROWS], x[ROWS:]], axis=1)

    def both_halves(h):
        pair = pl.ds(pl.multiple_of(h * PAIR, PAIR), PAIR)
        halves = range(TOKENS // ROWS)
        rows = [slice(half * ROWS, (half + 1) * ROWS) for half in halves]
        span = [slice(half * ROWS, half * ROWS + SPAN) for half in halves]
        cos = [jnp.concatenate([cosines[rows[half]]] * 2, axis=0) for half in halves]
        sin = [jnp.concatenate([sines[rows[half]]] * 2, axis=0) for half in halves]

        def score(half):
            raw = query_base[rows[half], pair].astype(F32) + dot(
                low_cols[rows[half]], query_up[:, pair], (1, 0)
            )
            queries = rope(stack(raw), cos[half], sin[half]) * (SCALE * math.log2(math.e))
            return dot(queries.astype(BF16), keys[h, span[half]], (1, 1))

        def attend(half, scores):
            scores = (
                scores.reshape(2, ROWS, SPAN) + bias[half][None]
            ).reshape(2 * ROWS, SPAN)
            weights = jnp.exp2(scores - jnp.max(scores, axis=1, keepdims=True))
            inverse = 1.0 / jnp.sum(weights, axis=1, keepdims=True)
            weights = weights.astype(BF16)
            result = (dot(weights, values[h, span[half]], (1, 0)) * inverse).astype(BF16)
            out[rows[half], pair] = beside(result)
            return weights, inverse, result

        def back(half, weights, inverse, result):
            out_grad = stack(gradient[rows[half], pair])
            grad_weights = dot(out_grad, values[h, span[half]], (1, 1))
            out_grad = out_grad.astype(F32)
            delta = jnp.sum(out_grad * result.astype(F32), axis=1, keepdims=True)
            terms = dot((out_grad * inverse).astype(BF16), weights, (0, 0))
            if half == 0:
                value_sum[:, 0:SPAN] = terms
            else:
                value_sum[:, ROWS:SPAN] += terms[:, : SPAN - ROWS]
                value_sum[:, SPAN:REACH] = terms[:, SPAN - ROWS :]
            grad_scores = weights * (grad_weights - delta).astype(BF16)
            turned = rope(
                dot(grad_scores, keys[h, span[half]], (1, 0)) * (inverse * SCALE),
                cos[half],
                -sin[half],
            )
            query_grad[rows[half]] = beside(turned.astype(BF16))

        scores = [score(half) for half in halves]
        attended = [attend(half, scores[half]) for half in halves]
        for half in halves:
            back(half, *attended[half])

    def absorb(h):
        @pl.when(ctx + 1 < count)
        def _():
            grad_copy(0, h).wait_recv()

        @pl.when(ctx + 2 < count)
        def _():
            grad_copy(1, h).wait_recv()

        total = (
            value_own[h] + value_got[h, 0].astype(F32) + value_got[h, 1].astype(F32)
        ).astype(BF16)
        columns = pl.ds(pl.multiple_of(h * HEAD_SIZE, HEAD_SIZE), HEAD_SIZE)
        back_mine[RANK : 2 * RANK] += dot(value_up[RANK : 2 * RANK, columns], total, (1, 0))
        row_value[:, pl.ds(pl.multiple_of(h * HEAD_SIZE, HEAD_SIZE) + FEATURES, HEAD_SIZE)] = dot(
            low_rows[RANK : 2 * RANK], total, (1, 1)
        )

    def one_head(h, carry):
        @pl.when(ctx >= 2)
        def _():
            far_copy(keys, 0, h).wait_recv()
            far_copy(values, 1, h).wait_recv()

        @pl.when((core == 1) & (ctx >= 2))
        def _():
            near_copy(keys, 0, h, 0, behind_1).start()
            near_copy(values, 1, h, 0, behind_1).start()

        @pl.when(h + AHEAD < KV)
        def _():
            send_own(keys, 0, h + AHEAD)
            send_own(values, 1, h + AHEAD)

        @pl.when(ctx >= 1)
        def _():
            near_copy(keys, 0, h, 0, behind_1).wait_recv()
            near_copy(values, 1, h, 0, behind_1).wait_recv()

        both_halves(h)
        value_sent[h, 1] = value_sum[:, 0:TOKENS].astype(BF16)
        value_sent[h, 0] = value_sum[:, TOKENS:WINDOW].astype(BF16)

        @pl.when(ctx >= 2)
        def _():
            grad_copy(1, h).start()

        @pl.when(ctx >= 1)
        def _():
            grad_copy(0, h).start()

        value_own[h] = value_sum[:, WINDOW:REACH]
        out_copy(h).start()
        pair = pl.ds(pl.multiple_of(h * PAIR, PAIR), PAIR)
        back_mine[0:RANK] += dot(query_up[0:RANK, pair], query_grad[...], (1, 1))
        row_query[:, pl.ds(pl.multiple_of(h * PAIR, HEAD_SIZE) + FEATURES, PAIR)] = dot(
            low_rows[0:RANK], query_grad[...], (1, 0)
        )

        @pl.when(h >= LAG)
        def _():
            absorb(h - LAG)

        return carry

    lax.fori_loop(0, KV, one_head, 0)

    def back_copy(kind):
        rows = pl.ds(kind * RANK, RANK)
        return remote(
            back_mine.at[rows],
            back_theirs.at[rows],
            back_sem.at[0, kind],
            back_sem.at[1, kind],
            ctx,
            1 - head,
        )

    stores = (
        (row_query, parts_query, near_query, away_query, final_query),
        (row_value, parts_value, near_value, away_value, final_value),
    )

    def sum_copy(kind, step, k, peer):
        _, parts, near, away, final = stores[kind]
        source, target = (
            (parts.at[peer % GROUP], near.at[k]),
            (away.at[group], away.at[group]),
            (final.at[member], final.at[member]),
        )[step]
        return remote(
            source, target, sum_send.at[kind, step, k], sum_recv.at[kind, step, k], peer
        )

    def sum_copies(kind, step):
        peers = far_peers if step == 1 else near_peers
        return [sum_copy(kind, step, k, peer) for k, peer in enumerate(peers)]

    def scatter(kind):
        row, parts = stores[kind][:2]
        rows = slice(kind * RANK, (kind + 1) * RANK)
        back_copy(kind).wait_recv()
        total = (back_mine[rows] + back_theirs[rows]).astype(BF16)
        row[:, 0:FEATURES] = dot(total, hidden[...], (1, 0))
        width = parts.shape[2]
        for k in range(GROUP):
            parts[k] = row[:, k * width : (k + 1) * width].astype(BF16)
        for one in sum_copies(kind, 0):
            one.start()

    def exchange(kind):
        _, parts, near, away, _ = stores[kind]
        total = parts[member].astype(F32)
        for k, one in enumerate(sum_copies(kind, 0)):
            one.wait_recv()
            total += near[k].astype(F32)
        away[group] = total.astype(BF16)
        for one in sum_copies(kind, 1):
            one.start()

    def gather(kind):
        away, final = stores[kind][3:]
        for one in sum_copies(kind, 1):
            one.wait_recv()
        total = away[0].astype(F32)
        for k in range(1, groups):
            total += away[k].astype(F32)
        final[member] = (total * (TOKENS * count) ** -0.5).astype(BF16)
        for one in sum_copies(kind, 2):
            one.start()

    back_copy(0).start()
    for h in range(KV - LAG, KV - 1):
        absorb(h)
    scatter(0)
    absorb(KV - 1)
    back_copy(1).start()
    exchange(0)
    scatter(1)
    gather(0)
    exchange(1)
    gather(1)
    low_copy.wait_send()
    for kind in range(2):
        for one in sum_copies(kind, 2):
            one.wait_recv()
        for step in range(3):
            for one in sum_copies(kind, step):
                one.wait_send()
        back_copy(kind).wait_send()

    def finish(h, carry):
        @pl.when(ctx + 2 < count)
        def _():
            far_copy(keys, 0, h).wait_send()
            far_copy(values, 1, h).wait_send()

        @pl.when((core == 0) | (ctx >= 2))
        def _():
            near_copy(keys, 0, h, 0, behind_1).wait_send()
            near_copy(values, 1, h, 0, behind_1).wait_send()

        @pl.when(ctx >= 1)
        def _():
            grad_copy(0, h).wait_send()

        @pl.when(ctx >= 2)
        def _():
            grad_copy(1, h).wait_send()

        out_copy(h).wait()
        return carry

    lax.fori_loop(0, KV, finish, 0)


def output_kernel(
    passed,
    final_query,
    final_value,
    attention_out,
    down_query,
    up_query,
    down_value,
    up_value,
    held,
    sem,
):
    size = TOKENS // PIECES

    def copy(k, step):
        piece = pl.ds(k * size, size)
        source, target = ((passed, held), (held, attention_out))[step]
        return pltpu.make_async_copy(source.at[piece], target.at[piece], sem.at[step, k])

    for k in range(PIECES):
        copy(k, 0).start()
    for k in range(PIECES):
        copy(k, 0).wait()
        copy(k, 1).start()
    for final, outs in ((final_query, (down_query, up_query)), (final_value, (down_value, up_value))):
        width = final.shape[2]
        for which, at, chunk, inside, size in pieces_of([o.shape[1] for o in outs], width):
            outs[which][:, at : at + size] = final[chunk, :, inside : inside + size].astype(F32)
    for k in range(PIECES):
        copy(k, 1).wait()


def per_device(
    hidden_states,
    query_base,
    key_base,
    frozen_value_rows,
    query_down,
    query_up,
    value_down,
    value_up_weight,
    positions,
    block_mask,
    output_gradient,
):
    anywhere = pl.BlockSpec(memory_space=pl.ANY)
    in_vmem = pl.BlockSpec(memory_space=pltpu.VMEM)
    columns = KV * HEAD_SIZE
    head_store = pltpu.VMEM((KV, REACH, HEAD_SIZE), BF16)
    value_terms = pltpu.VMEM((KV, 2, HEAD_SIZE, TOKENS), BF16)
    low_shape = pltpu.VMEM((2 * RANK, TOKENS), F32)
    query_sum = (GROUP, RANK, 5 * HEAD_SIZE)
    value_sum = (GROUP, RANK, 4 * HEAD_SIZE)
    dma = pltpu.SemaphoreType.DMA
    passed, final_query, final_value = pl.pallas_call(
        layer_kernel,
        out_shape=[
            jax.ShapeDtypeStruct((TOKENS, 2 * columns), BF16),
            jax.ShapeDtypeStruct(query_sum, BF16),
            jax.ShapeDtypeStruct(value_sum, BF16),
        ],
        in_specs=[anywhere] * 8
        + [in_vmem, in_vmem, pl.BlockSpec(memory_space=pltpu.SMEM), anywhere],
        out_specs=[anywhere, in_vmem, in_vmem],
        scratch_shapes=[
            pltpu.VMEM((TOKENS, FEATURES), BF16),
            pltpu.VMEM((TOKENS, 2 * columns), BF16),
            pltpu.VMEM((TOKENS, columns), BF16),
            pltpu.VMEM((TOKENS, columns), BF16),
            pltpu.VMEM((2 * RANK, FEATURES), BF16),
            pltpu.VMEM((2 * RANK, 2 * columns), BF16),
            pltpu.VMEM((2 * RANK, columns), BF16),
            pltpu.VMEM((TOKENS, 2 * columns), BF16),
            head_store,
            head_store,
            pltpu.VMEM((TOKENS, 2 * columns), BF16),
            pltpu.VMEM((TOKENS // ROWS, ROWS, SPAN), F32),
            pltpu.VMEM((TOKENS, HEAD_SIZE), F32),
            pltpu.VMEM((TOKENS, HEAD_SIZE), F32),
            low_shape,
            low_shape,
            pltpu.VMEM((2 * RANK, TOKENS), BF16),
            pltpu.VMEM((TOKENS, 2 * RANK), BF16),
            low_shape,
            low_shape,
            pltpu.VMEM((TOKENS, PAIR), BF16),
            pltpu.VMEM((HEAD_SIZE, REACH), F32),
            pltpu.VMEM((KV, HEAD_SIZE, TOKENS), F32),
            value_terms,
            value_terms,
            pltpu.VMEM((RANK, GROUP * query_sum[2]), F32),
            pltpu.VMEM((RANK, GROUP * value_sum[2]), F32),
        ]
        + [pltpu.VMEM(shape, BF16) for _ in range(3) for shape in (query_sum, value_sum)]
        + [
            dma((9,)),
            dma((KV,)),
            dma((2,)),
            dma((2, 2)),
        ]
        + [dma((2, KV))] * 6
        + [dma((2, 3, GROUP - 1))] * 2,
        compiler_params=pltpu.CompilerParams(
            collective_id=1, has_side_effects=True, vmem_limit_bytes=56 * 2**20
        ),
    )(
        hidden_states,
        query_base,
        key_base,
        frozen_value_rows,
        query_down.T,
        query_up,
        value_down.T,
        value_up_weight,
        positions.reshape(1, TOKENS),
        turns_of_angles(),
        block_mask.T,
        output_gradient,
    )
    outs = pl.pallas_call(
        output_kernel,
        out_shape=[
            jax.ShapeDtypeStruct((TOKENS, 2 * columns), BF16),
            jax.ShapeDtypeStruct((RANK, FEATURES), F32),
            jax.ShapeDtypeStruct((RANK, 2 * columns), F32),
            jax.ShapeDtypeStruct((RANK, FEATURES), F32),
            jax.ShapeDtypeStruct((RANK, columns), F32),
        ],
        in_specs=[anywhere, in_vmem, in_vmem],
        out_specs=[anywhere] + [in_vmem] * 4,
        scratch_shapes=[pltpu.VMEM((TOKENS, 2 * columns), BF16), dma((2, PIECES))],
        compiler_params=pltpu.CompilerParams(vmem_limit_bytes=56 * 2**20),
    )(passed, final_query, final_value)
    attention_out, down_query, up_query, down_value, up_value = outs
    return attention_out, down_query.T, up_query, down_value.T, up_value


def solution(mesh):
    placed = (
        P("ctx", "head"),
        P("ctx", "head"),
        P("ctx", "head"),
        P("ctx", "head"),
        P("head", None),
        P(None, "head"),
        P("head", None),
        P(None, "head"),
        P("ctx"),
        P(),
        P("ctx", "head"),
    )
    return jax.shard_map(
        per_device,
        mesh=mesh,
        in_specs=placed,
        out_specs=(
            P("ctx", "head"),
            P("head", None),
            P(None, "head"),
            P("head", None),
            P(None, "head"),
        ),
        check_vma=False,
    )
```

time: 116 us -> 105 us (0.905)
  local copies, waits for them, and re-layouts: 6.73 us -> 0 us
  Pallas kernels: 108 us -> 104 us
    pallas_call x1, Pallas kernels: 26.4 us -> 4.19 us  [per_device(): pl.pallas_call(output_kernel, out_shape=[jax.ShapeDtypeStruct((TOKENS, 2...]
    pallas_call x1, Pallas kernels: 81.8 us -> 99.9 us  [per_device(): pl.pallas_call(layer_kernel, out_shape=[jax.ShapeDtypeStruct((TOKENS, 2 *...]
    unnamed x7 -> x0, local copies, waits for them, and re-layouts: 6.73 us -> none
where the time goes in v3:
time: 105 us
  Pallas kernels  104 us (99%)
    pallas_call x1, Pallas kernels, per_device(): pl.pallas_call(layer_kernel, out_shape=[jax.ShapeDtypeStruct((TOKENS, 2 *...  99.9 us
    pallas_call x1, Pallas kernels, per_device(): pl.pallas_call(output_kernel, out_shape=[jax.ShapeDtypeStruct((TOKENS, 2...  4.19 us

profile of v3, /device:TPU:1, one launch (start us, length us, event | category | flops | bytes accessed | tf_op | source)
XLA Modules:
  0.0 104.7 jit_solution(12023989141405318701)
XLA Ops:
  0.6 99.9 %shard_map.155 = (bf16[512,2048]{1,0:T(8,128)(2,1)}, bf16[8,16,640]{2,1,0:T(8,128)(2,1)}, bf16[8,16,512]{2,1,0:T(8,128)(2,1)}) custom-call(bf16[512,2688]{1,0:T(8,128)(2,1)} %hidden_hbm.1, bf16[512,2048]{1,0:T(8,128)(2,1)} %query_hbm.1, bf16[512,1024]{1,0:T(8,128)(2,1)} %key_hbm.1, bf16[512,1024]{1,0:T(8,128)(2,1)} %value_hbm.1, bf16[16,2688]{1,0:T(8,128)(2,1)} %bitcast.6, ...), custom_call_target="tpu_custom_call" | custom-call | tf_op jit(solution)/shard_map/pallas_call | solution.py:609
  100.5 4.2 %shard_map.156 = (bf16[512,2048]{1,0:T(8,128)(2,1)}, f32[16,2688]{1,0:T(8,128)}, f32[16,2048]{1,0:T(8,128)}, f32[16,2688]{1,0:T(8,128)}, f32[16,1024]{1,0:T(8,128)}) custom-call(bf16[512,2048]{1,0:T(8,128)(2,1)} %get-tuple-element.13.passed, bf16[8,16,640]{2,1,0:T(8,128)(2,1)} %get-tuple-element.14.final_query, bf16[8,16,512]{2,1,0:T(8,128)(2,1)} %get-tuple-element.15.final_value), custom_call_target="tpu_custom_call" | custom-call | tf_op jit(solution)/shard_map/pallas_call | solution.py:674

commit v4 on v3

--- a/solution.py
+++ b/solution.py
@@ -24,7 +24,7 @@
 ROWS = 256
 SPAN = WINDOW + ROWS
 REACH = WINDOW + TOKENS
-AHEAD = 4
+AHEAD = 2
 LAG = 3
 HIDDEN = -1e30
 SCALE = (D // QUERY_HEADS) ** -0.5
@@ -116,6 +116,8 @@
     back_mine,
     back_theirs,
     query_grad,
+    held_weights,
+    held_inverse,
     value_sum,
     value_own,
     value_sent,
@@ -202,12 +204,15 @@
     def rope(x, cos, sin):
         return x * cos + pltpu.roll(x, HEAD_SIZE // 2, 1) * sin
 
-    loads[0].wait()
-    for h in range(KV):
+    def turn_keys(h):
         columns = slice(h * HEAD_SIZE, (h + 1) * HEAD_SIZE)
         keys[h, WINDOW:REACH] = rope(
             key_base[:, columns].astype(F32), cosines[...], sines[...]
         ).astype(BF16)
+
+    loads[0].wait()
+    for h in range(AHEAD):
+        turn_keys(h)
 
     pl.semaphore_wait(barrier, len(greeted))
 
@@ -246,6 +251,9 @@
     low_mine[...] = dot(downs[...], hidden[...], (1, 1))
     low_copy = remote(low_mine, low_theirs, low_sem.at[0], low_sem.at[1], ctx, 1 - head)
     low_copy.start()
+
+    for h in range(AHEAD, KV):
+        turn_keys(h)
 
     key_at = lax.broadcasted_iota(jnp.int32, (BLOCK, BLOCK), 1)
     query_at = lax.broadcasted_iota(jnp.int32, (BLOCK, BLOCK), 0)
@@ -302,7 +310,7 @@
         values[h, WINDOW:REACH] = (
             value_base[:, columns].astype(F32) + dot(low_cols[...], value_up[:, columns], (1, 0))
         ).astype(BF16)
-        if h < AHEAD:
+        if h < AHEAD - 1:
             send_own(values, 1, h)
     for one in loads[6:]:
         one.wait()
@@ -326,55 +334,110 @@
     def beside(x):
         return jnp.concatenate([x[:ROWS], x[ROWS:]], axis=1)
 
-    def both_halves(h):
-        pair = pl.ds(pl.multiple_of(h * PAIR, PAIR), PAIR)
-        halves = range(TOKENS // ROWS)
-        rows = [slice(half * ROWS, (half + 1) * ROWS) for half in halves]
-        span = [slice(half * ROWS, half * ROWS + SPAN) for half in halves]
-        cos = [jnp.concatenate([cosines[rows[half]]] * 2, axis=0) for half in halves]
-        sin = [jnp.concatenate([sines[rows[half]]] * 2, axis=0) for half in halves]
+    def send_terms(h):
+        value_sent[h, 1] = value_sum[:, 0:TOKENS].astype(BF16)
+        value_sent[h, 0] = value_sum[:, TOKENS:WINDOW].astype(BF16)
+
+        @pl.when(ctx >= 2)
+        def _():
+            grad_copy(1, h).start()
+
+        @pl.when(ctx >= 1)
+        def _():
+            grad_copy(0, h).start()
+
+        value_own[h] = value_sum[:, WINDOW:REACH]
+
+    halves = range(TOKENS // ROWS)
+    rows = [slice(half * ROWS, (half + 1) * ROWS) for half in halves]
+    span = [slice(half * ROWS, half * ROWS + SPAN) for half in halves]
+
+    def twice(x):
+        return jnp.concatenate([x, x], axis=0)
+
+    def pair_of(h):
+        return pl.ds(pl.multiple_of(h * PAIR, PAIR), PAIR)
+
+    def key_part(h):
+        pair = pair_of(h)
 
         def score(half):
             raw = query_base[rows[half], pair].astype(F32) + dot(
                 low_cols[rows[half]], query_up[:, pair], (1, 0)
             )
-            queries = rope(stack(raw), cos[half], sin[half]) * (SCALE * math.log2(math.e))
+            queries = rope(stack(raw), twice(cosines[rows[half]]), twice(sines[rows[half]]))
+            queries = queries * (SCALE * math.log2(math.e))
             return dot(queries.astype(BF16), keys[h, span[half]], (1, 1))
 
-        def attend(half, scores):
+        def weigh(half, scores):
             scores = (
                 scores.reshape(2, ROWS, SPAN) + bias[half][None]
             ).reshape(2 * ROWS, SPAN)
             weights = jnp.exp2(scores - jnp.max(scores, axis=1, keepdims=True))
             inverse = 1.0 / jnp.sum(weights, axis=1, keepdims=True)
             weights = weights.astype(BF16)
-            result = (dot(weights, values[h, span[half]], (1, 0)) * inverse).astype(BF16)
-            out[rows[half], pair] = beside(result)
-            return weights, inverse, result
-
-        def back(half, weights, inverse, result):
-            out_grad = stack(gradient[rows[half], pair])
-            grad_weights = dot(out_grad, values[h, span[half]], (1, 1))
-            out_grad = out_grad.astype(F32)
-            delta = jnp.sum(out_grad * result.astype(F32), axis=1, keepdims=True)
+            held_weights[h % 2, half] = weights
+            held_inverse[h % 2, half] = jnp.broadcast_to(inverse, (2 * ROWS, HEAD_SIZE))
+            out_grad = stack(gradient[rows[half], pair]).astype(F32)
             terms = dot((out_grad * inverse).astype(BF16), weights, (0, 0))
             if half == 0:
                 value_sum[:, 0:SPAN] = terms
             else:
                 value_sum[:, ROWS:SPAN] += terms[:, : SPAN - ROWS]
                 value_sum[:, SPAN:REACH] = terms[:, SPAN - ROWS :]
-            grad_scores = weights * (grad_weights - delta).astype(BF16)
+
+        scores = [score(half) for half in halves]
+        for half in halves:
+            weigh(half, scores[half])
+        send_terms(h)
+
+    def value_part(h):
+        pair = pair_of(h)
+
+        def attend(half):
+            result = dot(held_weights[h % 2, half], values[h, span[half]], (1, 0))
+            result = (result * held_inverse[h % 2, half]).astype(BF16)
+            out[rows[half], pair] = beside(result)
+            return result
+
+        def grad(half):
+            return dot(stack(gradient[rows[half], pair]), values[h, span[half]], (1, 1))
+
+        def back(half, grad_weights, result):
+            out_grad = stack(gradient[rows[half], pair]).astype(F32)
+            delta = jnp.sum(out_grad * result.astype(F32), axis=1, keepdims=True)
+            grad_scores = held_weights[h % 2, half] * (grad_weights - delta).astype(BF16)
             turned = rope(
-                dot(grad_scores, keys[h, span[half]], (1, 0)) * (inverse * SCALE),
-                cos[half],
-                -sin[half],
+                dot(grad_scores, keys[h, span[half]], (1, 0))
+                * (held_inverse[h % 2, half] * SCALE),
+                twice(cosines[rows[half]]),
+                -twice(sines[rows[half]]),
             )
             query_grad[rows[half]] = beside(turned.astype(BF16))
 
-        scores = [score(half) for half in halves]
-        attended = [attend(half, scores[half]) for half in halves]
+        results = [attend(half) for half in halves]
+        grads = [grad(half) for half in halves]
         for half in halves:
-            back(half, *attended[half])
+            back(half, grads[half], results[half])
+        out_copy(h).start()
+        back_mine[0:RANK] += dot(query_up[0:RANK, pair], query_grad[...], (1, 1))
+        row_query[:, pl.ds(pl.multiple_of(h * PAIR, HEAD_SIZE) + FEATURES, PAIR)] = dot(
+            low_rows[0:RANK], query_grad[...], (1, 0)
+        )
+
+    def pass_on(store, kind, h):
+        @pl.when(ctx >= 2)
+        def _():
+            far_copy(store, kind, h).wait_recv()
+
+        @pl.when((core == 1) & (ctx >= 2))
+        def _():
+            near_copy(store, kind, h, 0, behind_1).start()
+
+    def arrived(store, kind, h):
+        @pl.when(ctx >= 1)
+        def _():
+            near_copy(store, kind, h, 0, behind_1).wait_recv()
 
     def absorb(h):
         @pl.when(ctx + 1 < count)
@@ -395,45 +458,23 @@
         )
 
     def one_head(h, carry):
-        @pl.when(ctx >= 2)
-        def _():
-            far_copy(keys, 0, h).wait_recv()
-            far_copy(values, 1, h).wait_recv()
-
-        @pl.when((core == 1) & (ctx >= 2))
-        def _():
-            near_copy(keys, 0, h, 0, behind_1).start()
-            near_copy(values, 1, h, 0, behind_1).start()
-
         @pl.when(h + AHEAD < KV)
         def _():
             send_own(keys, 0, h + AHEAD)
-            send_own(values, 1, h + AHEAD)
-
-        @pl.when(ctx >= 1)
-        def _():
-            near_copy(keys, 0, h, 0, behind_1).wait_recv()
-            near_copy(values, 1, h, 0, behind_1).wait_recv()
-
-        both_halves(h)
-        value_sent[h, 1] = value_sum[:, 0:TOKENS].astype(BF16)
-        value_sent[h, 0] = value_sum[:, TOKENS:WINDOW].astype(BF16)
-
-        @pl.when(ctx >= 2)
-        def _():
-            grad_copy(1, h).start()
-
-        @pl.when(ctx >= 1)
-        def _():
-            grad_copy(0, h).start()
-
-        value_own[h] = value_sum[:, WINDOW:REACH]
-        out_copy(h).start()
-        pair = pl.ds(pl.multiple_of(h * PAIR, PAIR), PAIR)
-        back_mine[0:RANK] += dot(query_up[0:RANK, pair], query_grad[...], (1, 1))
-        row_query[:, pl.ds(pl.multiple_of(h * PAIR, HEAD_SIZE) + FEATURES, PAIR)] = dot(
-            low_rows[0:RANK], query_grad[...], (1, 0)
-        )
+
+        @pl.when(h + AHEAD - 1 < KV)
+        def _():
+            send_own(values, 1, h + AHEAD - 1)
+
+        pass_on(keys, 0, h)
+        arrived(keys, 0, h)
+        key_part(h)
+
+        @pl.when(h >= 1)
+        def _():
+            pass_on(values, 1, h - 1)
+            arrived(values, 1, h - 1)
+            value_part(h - 1)
 
         @pl.when(h >= LAG)
         def _():
@@ -442,6 +483,7 @@
         return carry
 
     lax.fori_loop(0, KV, one_head, 0)
+    pass_on(values, 1, KV - 1)
 
     def back_copy(kind):
         rows = pl.ds(kind * RANK, RANK)
@@ -507,16 +549,18 @@
         for one in sum_copies(kind, 2):
             one.start()
 
-    back_copy(0).start()
     for h in range(KV - LAG, KV - 1):
         absorb(h)
-    scatter(0)
+    arrived(values, 1, KV - 1)
+    value_part(KV - 1)
+    back_copy(0).start()
     absorb(KV - 1)
     back_copy(1).start()
+    scatter(0)
+    scatter(1)
     exchange(0)
-    scatter(1)
+    exchange(1)
     gather(0)
-    exchange(1)
     gather(1)
     low_copy.wait_send()
     for kind in range(2):
@@ -638,6 +682,8 @@
             low_shape,
             low_shape,
             pltpu.VMEM((TOKENS, PAIR), BF16),
+            pltpu.VMEM((2, TOKENS // ROWS, 2 * ROWS, SPAN), BF16),
+            pltpu.VMEM((2, TOKENS // ROWS, 2 * ROWS, HEAD_SIZE), F32),
             pltpu.VMEM((HEAD_SIZE, REACH), F32),
             pltpu.VMEM((KV, HEAD_SIZE, TOKENS), F32),
             value_terms,

time: 105 us -> 90.6 us (0.86)
  Pallas kernels: 104 us -> 89.7 us
    pallas_call x1, Pallas kernels: 99.9 us -> 85.6 us  [per_device(): pl.pallas_call(layer_kernel, out_shape=[jax.ShapeDtypeStruct((TOKENS, 2 *...]
where the time goes in v4:
time: 90.6 us; the launch traced here: 90.4 us
  Pallas kernels  89.7 us (99%)
    pallas_call x1, Pallas kernels, per_device(): pl.pallas_call(layer_kernel, out_shape=[jax.ShapeDtypeStruct((TOKENS, 2 *...  85.6 us
    pallas_call x1, Pallas kernels, per_device(): pl.pallas_call(output_kernel, out_shape=[jax.ShapeDtypeStruct((TOKENS, 2...  4.19 us

profile of v4, /device:TPU:1, one launch (start us, length us, event | category | flops | bytes accessed | tf_op | source)
XLA Modules:
  0.0 90.4 jit_solution(2457484046280399098)
XLA Ops:
  0.6 85.6 %shard_map.155 = (bf16[512,2048]{1,0:T(8,128)(2,1)}, bf16[8,16,640]{2,1,0:T(8,128)(2,1)}, bf16[8,16,512]{2,1,0:T(8,128)(2,1)}) custom-call(bf16[512,2688]{1,0:T(8,128)(2,1)} %hidden_hbm.1, bf16[512,2048]{1,0:T(8,128)(2,1)} %query_hbm.1, bf16[512,1024]{1,0:T(8,128)(2,1)} %key_hbm.1, bf16[512,1024]{1,0:T(8,128)(2,1)} %value_hbm.1, bf16[16,2688]{1,0:T(8,128)(2,1)} %bitcast.6, ...), custom_call_target="tpu_custom_call" | custom-call | tf_op jit(solution)/shard_map/pallas_call | solution.py:653
  86.2 4.2 %shard_map.156 = (bf16[512,2048]{1,0:T(8,128)(2,1)}, f32[16,2688]{1,0:T(8,128)}, f32[16,2048]{1,0:T(8,128)}, f32[16,2688]{1,0:T(8,128)}, f32[16,1024]{1,0:T(8,128)}) custom-call(bf16[512,2048]{1,0:T(8,128)(2,1)} %get-tuple-element.13.passed, bf16[8,16,640]{2,1,0:T(8,128)(2,1)} %get-tuple-element.14.final_query, bf16[8,16,512]{2,1,0:T(8,128)(2,1)} %get-tuple-element.15.final_value), custom_call_target="tpu_custom_call" | custom-call | tf_op jit(solution)/shard_map/pallas_call | solution.py:720

commit v5 on v4

--- a/solution.py
+++ b/solution.py
@@ -606,7 +606,15 @@
     down_value,
     up_value,
     held,
+    sums_query,
+    sums_value,
+    wide_0,
+    wide_1,
+    wide_2,
+    wide_3,
     sem,
+    sums_sem,
+    wide_sem,
 ):
     size = TOKENS // PIECES
 
@@ -615,17 +623,38 @@
         source, target = ((passed, held), (held, attention_out))[step]
         return pltpu.make_async_copy(source.at[piece], target.at[piece], sem.at[step, k])
 
+    sums = [
+        pltpu.make_async_copy(final_query, sums_query, sums_sem.at[0]),
+        pltpu.make_async_copy(final_value, sums_value, sums_sem.at[1]),
+    ]
+    for one in sums:
+        one.start()
     for k in range(PIECES):
         copy(k, 0).start()
+    written = []
+    for kind, (final, wides, outs) in enumerate(
+        (
+            (sums_query, (wide_0, wide_1), (down_query, up_query)),
+            (sums_value, (wide_2, wide_3), (down_value, up_value)),
+        )
+    ):
+        sums[kind].wait()
+        width = final.shape[2]
+        for which, at, chunk, inside, part in pieces_of([o.shape[1] for o in outs], width):
+            wides[which][:, at : at + part] = final[chunk, :, inside : inside + part].astype(F32)
+        for which in range(2):
+            one = pltpu.make_async_copy(
+                wides[which], outs[which], wide_sem.at[2 * kind + which]
+            )
+            one.start()
+            written.append(one)
     for k in range(PIECES):
         copy(k, 0).wait()
         copy(k, 1).start()
-    for final, outs in ((final_query, (down_query, up_query)), (final_value, (down_value, up_value))):
-        width = final.shape[2]
-        for which, at, chunk, inside, size in pieces_of([o.shape[1] for o in outs], width):
-            outs[which][:, at : at + size] = final[chunk, :, inside : inside + size].astype(F32)
     for k in range(PIECES):
         copy(k, 1).wait()
+    for one in written:
+        one.wait()
 
 
 def per_device(
@@ -726,9 +755,15 @@
             jax.ShapeDtypeStruct((RANK, FEATURES), F32),
             jax.ShapeDtypeStruct((RANK, columns), F32),
         ],
-        in_specs=[anywhere, in_vmem, in_vmem],
-        out_specs=[anywhere] + [in_vmem] * 4,
-        scratch_shapes=[pltpu.VMEM((TOKENS, 2 * columns), BF16), dma((2, PIECES))],
+        in_specs=[anywhere] * 3,
+        out_specs=[anywhere] * 5,
+        scratch_shapes=[
+            pltpu.VMEM((TOKENS, 2 * columns), BF16),
+            pltpu.VMEM(query_sum, BF16),
+            pltpu.VMEM(value_sum, BF16),
+        ]
+        + [pltpu.VMEM((RANK, width), F32) for width in (FEATURES, 2 * columns, FEATURES, columns)]
+        + [dma((2, PIECES)), dma((2,)), dma((4,))],
         compiler_params=pltpu.CompilerParams(vmem_limit_bytes=56 * 2**20),
     )(passed, final_query, final_value)
     attention_out, down_query, up_query, down_value, up_value = outs

time: 90.6 us -> 89.4 us (0.987)
  Pallas kernels: 89.7 us -> 88.5 us
    pallas_call x1, Pallas kernels: 4.19 us -> 2.96 us  [per_device(): pl.pallas_call(output_kernel, out_shape=[jax.ShapeDtypeStruct((TOKENS, 2...]
where the time goes in v5:
time: 89.4 us; the launch traced here: 89.2 us
  Pallas kernels  88.5 us (99%)
    pallas_call x1, Pallas kernels, per_device(): pl.pallas_call(layer_kernel, out_shape=[jax.ShapeDtypeStruct((TOKENS, 2 *...  85.6 us
    pallas_call x1, Pallas kernels, per_device(): pl.pallas_call(output_kernel, out_shape=[jax.ShapeDtypeStruct((TOKENS, 2...  2.96 us

profile of v5, /device:TPU:1, one launch (start us, length us, event | category | flops | bytes accessed | tf_op | source)
XLA Modules:
  0.0 89.2 jit_solution(5241226070088277543)
XLA Ops:
  0.6 85.6 %shard_map.155 = (bf16[512,2048]{1,0:T(8,128)(2,1)}, bf16[8,16,640]{2,1,0:T(8,128)(2,1)}, bf16[8,16,512]{2,1,0:T(8,128)(2,1)}) custom-call(bf16[512,2688]{1,0:T(8,128)(2,1)} %hidden_hbm.1, bf16[512,2048]{1,0:T(8,128)(2,1)} %query_hbm.1, bf16[512,1024]{1,0:T(8,128)(2,1)} %key_hbm.1, bf16[512,1024]{1,0:T(8,128)(2,1)} %value_hbm.1, bf16[16,2688]{1,0:T(8,128)(2,1)} %bitcast.6, ...), custom_call_target="tpu_custom_call" | custom-call | tf_op jit(solution)/shard_map/pallas_call | solution.py:682
  86.2 3.0 %shard_map.156 = (bf16[512,2048]{1,0:T(8,128)(2,1)}, f32[16,2688]{1,0:T(8,128)}, f32[16,2048]{1,0:T(8,128)}, f32[16,2688]{1,0:T(8,128)}, f32[16,1024]{1,0:T(8,128)}) custom-call(bf16[512,2048]{1,0:T(8,128)(2,1)} %get-tuple-element.13.passed, bf16[8,16,640]{2,1,0:T(8,128)(2,1)} %get-tuple-element.14.final_query, bf16[8,16,512]{2,1,0:T(8,128)(2,1)} %get-tuple-element.15.final_value), custom_call_target="tpu_custom_call" | custom-call | tf_op jit(solution)/shard_map/pallas_call | solution.py:749

commit v6 on v5

--- a/solution.py
+++ b/solution.py
@@ -551,17 +551,17 @@
 
     for h in range(KV - LAG, KV - 1):
         absorb(h)
+    absorb(KV - 1)
+    back_copy(1).start()
     arrived(values, 1, KV - 1)
     value_part(KV - 1)
     back_copy(0).start()
-    absorb(KV - 1)
-    back_copy(1).start()
+    scatter(1)
     scatter(0)
-    scatter(1)
+    exchange(1)
     exchange(0)
-    exchange(1)
+    gather(1)
     gather(0)
-    gather(1)
     low_copy.wait_send()
     for kind in range(2):
         for one in sum_copies(kind, 2):

time: 89.4 us -> 91.9 us (1.028)
  Pallas kernels: 88.5 us -> 91 us
    pallas_call x1, Pallas kernels: 85.6 us -> 88.1 us  [per_device(): pl.pallas_call(layer_kernel, out_shape=[jax.ShapeDtypeStruct((TOKENS, 2 *...]
where the time goes in v6:
time: 91.9 us; the launch traced here: 91.7 us
  Pallas kernels  91 us (99%)
    pallas_call x1, Pallas kernels, per_device(): pl.pallas_call(layer_kernel, out_shape=[jax.ShapeDtypeStruct((TOKENS, 2 *...  88.1 us
    pallas_call x1, Pallas kernels, per_device(): pl.pallas_call(output_kernel, out_shape=[jax.ShapeDtypeStruct((TOKENS, 2...  2.96 us

profile of v6, /device:TPU:1, one launch (start us, length us, event | category | flops | bytes accessed | tf_op | source)
XLA Modules:
  0.0 91.7 jit_solution(2625616916829501219)
XLA Ops:
  0.6 88.1 %shard_map.155 = (bf16[512,2048]{1,0:T(8,128)(2,1)}, bf16[8,16,640]{2,1,0:T(8,128)(2,1)}, bf16[8,16,512]{2,1,0:T(8,128)(2,1)}) custom-call(bf16[512,2688]{1,0:T(8,128)(2,1)} %hidden_hbm.1, bf16[512,2048]{1,0:T(8,128)(2,1)} %query_hbm.1, bf16[512,1024]{1,0:T(8,128)(2,1)} %key_hbm.1, bf16[512,1024]{1,0:T(8,128)(2,1)} %value_hbm.1, bf16[16,2688]{1,0:T(8,128)(2,1)} %bitcast.6, ...), custom_call_target="tpu_custom_call" | custom-call | tf_op jit(solution)/shard_map/pallas_call | solution.py:682
  88.7 3.0 %shard_map.156 = (bf16[512,2048]{1,0:T(8,128)(2,1)}, f32[16,2688]{1,0:T(8,128)}, f32[16,2048]{1,0:T(8,128)}, f32[16,2688]{1,0:T(8,128)}, f32[16,1024]{1,0:T(8,128)}) custom-call(bf16[512,2048]{1,0:T(8,128)(2,1)} %get-tuple-element.13.passed, bf16[8,16,640]{2,1,0:T(8,128)(2,1)} %get-tuple-element.14.final_query, bf16[8,16,512]{2,1,0:T(8,128)(2,1)} %get-tuple-element.15.final_value), custom_call_target="tpu_custom_call" | custom-call | tf_op jit(solution)/shard_map/pallas_call | solution.py:749
